TPU v7x, 32 devices: a whole 2x2x4 slice. The times are simulated.
32 devices in a mesh: groups: 2 (over y), pool: 4 (over z), tensor: 2 (over x), sub: 2 (over core).
Axes of the slice: x: 2, y: 2, z: 4, core: 2. Of those that a mesh axis runs over, the one named last changes fastest.
Arguments:
- queries: bfloat16 [8, 160, 8192], P(('groups', 'pool'), None, ('tensor', 'sub')), parts along dimension 0, may hold values from -16 to 16
- new_keys: bfloat16 [8, 160, 1024], P(('groups', 'pool'), None, ('tensor', 'sub')), parts along dimension 0, may hold values from -9.6 to 9.6
- new_values: bfloat16 [8, 160, 1024], P(('groups', 'pool'), None, ('tensor', 'sub')), parts along dimension 0, may hold values from -6 to 6
- store_keys: bfloat16 [256, 256, 1024], P(('groups', 'pool'), None, ('tensor', 'sub')), parts along dimension 0, may hold values from -9.5625 to 9.5625
- store_values: bfloat16 [256, 256, 1024], P(('groups', 'pool'), None, ('tensor', 'sub')), parts along dimension 0, may hold values from -6 to 6
- prefix_blocks: int32 [8], P('groups'), parts along dimension 0, may hold values from 8 to 32, as said below
- hit_store: int32 [8, 32], P('groups'), parts along dimension 0, may hold values from 0 to 3, as said below
- hit_slot: int32 [8, 32], P('groups'), parts along dimension 0, may hold values from 0 to 31, as said below
- decode_owner: int32 [8], P('groups'), parts along dimension 0, may hold values from 0 to 3, as said below
Outputs:
- attended: bfloat16 [8, 160, 8192], P(('groups', 'pool'), None, ('tensor', 'sub')), parts along dimension 0
- pushed_keys: bfloat16 [16, 160, 1024], P(('groups', 'pool'), None, ('tensor', 'sub')), parts along dimension 0
- pushed_values: bfloat16 [16, 160, 1024], P(('groups', 'pool'), None, ('tensor', 'sub')), parts along dimension 0
There are 2 independent parts, one for each index of `groups`. A program takes and returns all parts, laid end to end along the dimension named above; each array names one. Nothing has to cross between parts.
Inputs may be any that keep to these rules, and one draw needn't show every extreme that they name: `prefix_blocks`: some request has exactly 32 cached blocks. `hit_store`: consecutive blocks of a request lie on store devices of consecutive index, wrapping around, so one store device holds at most 8 blocks of a request, and the request with 32 blocks puts exactly 8 on some store device. Entries past a request's count mean nothing. `hit_slot`: the cached blocks held by one store device occupy distinct slots. Entries past a request's count mean nothing. `decode_owner`: no instance decodes more than 2 requests, and some instance decodes exactly 2.
All inputs are finite; a program needn't handle non-finite values.
Results may differ from a plain program's by a relative error of at most 0.004.
Values may be sent and summed in bfloat16 or wider, within the bound.
No kernel may reach another device: no remote copies, remote signals or barrier semaphores. Data moves between devices by JAX's collectives and lax.ppermute only.
A program may use at most 128 MiB of HBM per device.

v0:
```python
import functools
import math

import jax
import jax.numpy as jnp
from jax import lax
from jax.experimental import pallas as pl
from jax.experimental.pallas import tpu as pltpu
from jax.sharding import PartitionSpec as P

HEADS = 64
KVH = 8
HD = 128
MAXBLK = 32
CAPP = 2
GROUP = HEADS // KVH
EMPTY = -1e30
TILE = 256
ONES = 16
PIECE = 32
EXP2_SCALE = math.log2(math.e) / math.sqrt(HD)
VMEM_LIMIT = 63 * 1024 * 1024 + 512 * 1024


def blocks_at(tables, request, place, pool_size):
    prefix_ref, store_ref, slot_ref = tables
    first = lax.rem(place - store_ref[request, 0] + pool_size, pool_size)
    count = lax.max(lax.div(prefix_ref[request] - first + pool_size - 1, pool_size), 0)
    return count, lambda entry: slot_ref[request, first + entry * pool_size]


def fetch(pool_size, tables, request, stores, buffers, sems, moved=None):
    me = lax.axis_index("pool")
    count, slot_of = blocks_at(tables, request, me if moved is None else me ^ 1, pool_size)

    def copies(entry):
        for i in range(2):
            if moved is None:
                source = stores[i].at[slot_of(entry)]
            else:
                source = moved.at[i * (moved.shape[0] // 2) + entry]
            yield pltpu.make_async_copy(source, buffers[i].at[entry], sems.at[i, entry])

    def start(entry, carry):
        for copy in copies(entry):
            copy.start()
        return carry

    lax.fori_loop(0, count, start, 0)

    def ready(entry):
        for copy in copies(entry):
            copy.wait()

    return count, ready


def gather_kernel(pool_size, prefix_ref, store_ref, slot_ref, store_keys, store_values, out_ref, sems):
    me = lax.axis_index("pool")
    capacity = out_ref.shape[0] // 2

    @pl.when(jnp.logical_not(is_inner(me)))
    def _():
        tables = (prefix_ref, store_ref, slot_ref)
        count, slot_of = blocks_at(tables, me ^ 3, me, pool_size)

        def copies(entry):
            return [
                pltpu.make_async_copy(
                    store.at[slot_of(entry)], out_ref.at[i * capacity + entry], sems.at[i, entry]
                )
                for i, store in enumerate((store_keys, store_values))
            ]

        def start(entry, carry):
            for copy in copies(entry):
                copy.start()
            return carry

        def wait(entry, carry):
            for copy in copies(entry):
                copy.wait()
            return carry

        lax.fori_loop(0, count, start, 0)
        lax.fori_loop(0, count, wait, 0)


def attend(
    key_ref,
    value_ref,
    count,
    ready,
    fresh,
    new_rows,
    columns,
    scores,
    weights,
    peaks,
    factors,
    tops,
    turned,
    acc,
    initial=None,
    raw=False,
):
    rows = columns.shape[1]
    kv_local = columns.shape[0] // HD

    def visit(keys, values, seen):
        size = keys[0].shape[0]

        def score(kv):
            turned[kv, :HD, :size] = values[kv].T
            block = lax.dot_general(
                keys[kv],
                columns[kv * HD : (kv + 1) * HD, :],
                (((1,), (0,)), ((), ())),
                preferred_element_type=jnp.float32,
            )
            block = block * EXP2_SCALE
            if seen is not None:
                block = jnp.where(seen, block, EMPTY)
            scores[kv, :size, :] = block
            tops[kv] = jnp.max(block.reshape(size // 8, 8, rows), axis=0)

        def weigh(kv):
            for i in range(0, rows, TILE):
                part = slice(i, i + TILE)
                before = peaks[kv, :, part]
                top = jnp.max(tops[kv, :, part], axis=0, keepdims=True)
                peak = jnp.maximum(before, top)
                factors[kv, :, part] = jnp.exp2(before - peak)
                peaks[kv, :, part] = peak
                weight = jnp.exp2(scores[kv, :size, part] - peak[0:1])
                weights[kv, :size, part] = weight.astype(jnp.bfloat16)

        def mix(kv):
            added = lax.dot_general(
                turned[kv, :, :size],
                weights[kv, :size, :],
                (((1,), (0,)), ((), ())),
                preferred_element_type=jnp.float32,
            )
            acc[kv] = acc[kv] * factors[kv, 0:1, :] + added

        for step in range(kv_local + 2):
            for offset, stage in ((0, score), (2, mix), (1, weigh)):
                if 0 <= step - offset < kv_local:
                    stage(step - offset)

    def lanes_of(array):
        return [array[:, kv * HD : (kv + 1) * HD] for kv in range(kv_local)]

    def blocks_of(ref, first, number):
        return lanes_of(ref[pl.ds(first, number)].reshape(number * ref.shape[1], ref.shape[2]))

    if initial is None:
        peaks[...] = jnp.full(peaks.shape, EMPTY, jnp.float32)
        acc[...] = jnp.zeros(acc.shape, jnp.float32)
    else:
        for copy in initial(acc, peaks):
            copy.wait()
    turned[:, HD:, :] = jnp.ones((kv_local, ONES, turned.shape[2]), jnp.bfloat16)
    if fresh is not None:
        new_key_ref, new_value_ref = fresh
        row = lax.rem(lax.broadcasted_iota(jnp.int32, (1, rows), 1), new_rows)
        seen = lax.broadcasted_iota(jnp.int32, (new_key_ref.shape[0], rows), 0) <= row
        visit(lanes_of(new_key_ref), lanes_of(new_value_ref), seen)

    def visit_blocks(number):
        def body(index, carry):
            for i in range(number):
                ready(index * number + i)
            visit(
                blocks_of(key_ref, index * number, number),
                blocks_of(value_ref, index * number, number),
                None,
            )
            return carry

        return body

    pairs = count // 2 if key_ref.shape[0] > 1 else 0
    if key_ref.shape[0] > 1:
        lax.fori_loop(0, pairs, visit_blocks(2), 0)
    lax.fori_loop(2 * pairs, count, visit_blocks(1), 0)
    if raw:
        return acc, peaks
    outs = []
    logs = []
    for kv in range(kv_local):
        total = acc[kv, HD : HD + 1, :]
        safe = jnp.where(total > 0, total, 1.0)
        logs.append(jnp.where(total > 0, peaks[kv, 0:1] * math.log(2.0) + jnp.log(safe), EMPTY))
        outs.append(acc[kv, :HD, :] * (1.0 / safe))
    return outs, logs


def prepare_kernel(query_ref, new_key_ref, new_value_ref, payload_ref, query_rows):
    new_rows = query_ref.shape[0]
    kv_width = new_key_ref.shape[1]
    for kv in range(kv_width // HD):
        for g in range(GROUP):
            head = kv * GROUP + g
            query_rows[g * new_rows : (g + 1) * new_rows, :] = query_ref[
                :, head * HD : (head + 1) * HD
            ]
        payload_ref[kv * HD : (kv + 1) * HD, :] = query_rows[...].T
    for i, new_ref in enumerate((new_key_ref, new_value_ref)):
        for piece in range(new_rows // PIECE):
            row, lane = piece_place(i, piece, new_rows, kv_width)
            payload_ref[row : row + PIECE, lane : lane + kv_width] = new_ref[
                piece * PIECE : (piece + 1) * PIECE, :
            ]


def piece_place(i, piece, new_rows, kv_width):
    index = i * (new_rows // PIECE) + piece
    beside = GROUP * new_rows // kv_width
    return kv_width + index // beside * PIECE, index % beside * kv_width


def payload_rows(new_rows, kv_width):
    return piece_place(1, new_rows // PIECE - 1, new_rows, kv_width)[0] + PIECE


def own_kernel(
    pool_size,
    prefix_ref,
    store_ref,
    slot_ref,
    payload_ref,
    new_key_ref,
    new_value_ref,
    store_keys,
    store_values,
    out_ref,
    log_ref,
    key_buf,
    value_buf,
    new_key_buf,
    new_value_buf,
    *state,
):
    *work, sems = state
    count, ready = fetch(
        pool_size,
        (prefix_ref, store_ref, slot_ref),
        lax.axis_index("pool"),
        (store_keys, store_values),
        (key_buf, value_buf),
        sems,
    )
    new_rows, kv_width = new_key_ref.shape
    for buffer, source in ((new_key_buf, new_key_ref), (new_value_buf, new_value_ref)):
        buffer[:new_rows, :] = source[...]
        buffer[new_rows:, :] = jnp.zeros((buffer.shape[0] - new_rows, kv_width), jnp.bfloat16)
    fresh = (new_key_buf, new_value_buf)
    outs, logs = attend(
        key_buf, value_buf, count, ready, fresh, new_rows, payload_ref.at[:kv_width], *work
    )
    log_ref[...] = jnp.zeros(log_ref.shape, jnp.float32)
    for kv, (out, log) in enumerate(zip(outs, logs)):
        out_ref[kv * HD : (kv + 1) * HD, :] = out
        log_ref[kv : kv + 1, :] = log


def other_kernel(pool_size, new_rows, partners, with_moved, raw, *refs):
    if partners is None:
        request = refs[0][0]
        choice = [None]
        refs = refs[1:]
    else:
        inner = is_inner(lax.axis_index("pool"))
        _, request = source_of(lax.axis_index("pool"), partners)
        choice = [
            hit for hit, mask in zip((inner, jnp.logical_not(inner)), partners) if mask is not None
        ]
    tables, refs = refs[:3], refs[3:]
    payload_refs, refs = refs[: len(choice)], refs[len(choice) :]
    moved = initial = None
    if with_moved:
        moved, *initial = refs[:3]
        refs = refs[3:]
    store_keys, store_values, *refs = refs
    results_ref, (key_buf, value_buf, *state) = refs[: 1 + raw], refs[1 + raw :]
    *work, columns, query_sem, out_buf, out_sem, sems = state
    kv_width = columns.shape[0]

    def query_copy(payload_ref):
        return pltpu.make_async_copy(payload_ref.at[:kv_width], columns, query_sem)

    def run():
        for payload_ref, hit in zip(payload_refs, choice):
            if len(choice) == 1:
                query_copy(payload_ref).start()
            else:
                pl.when(hit)(query_copy(payload_ref).start)
        count, ready = fetch(
            pool_size,
            tables,
            request,
            (store_keys, store_values),
            (key_buf, value_buf),
            sems,
            moved,
        )
        restore = None
        if initial is not None:

            def restore(*targets):
                return [
                    pltpu.make_async_copy(source, target, out_sem.at[i])
                    for i, (source, target) in enumerate(zip(initial, targets))
                ]

            for copy in restore(work[-1], work[2]):
                copy.start()
        query_copy(payload_refs[0]).wait()
        results = attend(
            key_buf, value_buf, count, ready, None, new_rows, columns, *work, restore, raw
        )
        if raw:
            copies = [
                pltpu.make_async_copy(result, out_ref, out_sem.at[i])
                for i, (out_ref, result) in enumerate(zip(results_ref, results))
            ]
            for copy in copies:
                copy.start()
            for copy in copies:
                copy.wait()
            return
        outs, logs = results
        tail = []
        copies = []

        def send_rows(start, size):
            copies.append(
                pltpu.make_async_copy(
                    out_buf.at[start : start + size],
                    results_ref[0].at[start : start + size],
                    out_sem.at[len(copies)],
                )
            )
            copies[-1].start()

        for kv, (out, log) in enumerate(zip(outs, logs)):
            out_buf[kv * HD : (kv + 1) * HD, :] = out.astype(jnp.bfloat16)
            send_rows(kv * HD, HD)
            high = log.astype(jnp.bfloat16).astype(jnp.float32)
            middle = (log - high).astype(jnp.bfloat16).astype(jnp.float32)
            tail += [high, middle, log - high - middle]
        tail.append(jnp.zeros((ONES - len(tail), columns.shape[1]), jnp.float32))
        out_buf[kv_width:, :] = jnp.concatenate(tail, axis=0).astype(jnp.bfloat16)
        send_rows(kv_width, ONES)
        for copy in copies:
            copy.wait()

    if len(choice) == 1 and choice[0] is not None:
        pl.when(choice[0])(run)
    else:
        run()


def is_inner(place):
    return (place == 1) | (place == 2)


def source_of(me, entry):
    if isinstance(entry, int):
        return jnp.bool_(True), jnp.int32(entry)
    inner = is_inner(me)
    masks = [0 if mask is None else mask for mask in entry]
    there = jnp.where(inner, entry[0] is not None, entry[1] is not None)
    return there, me ^ jnp.where(inner, masks[0], masks[1])


def push_kernel(pool_size, entries, owner_ref, *refs):
    payload_refs = refs[: len(entries)]
    key_out, value_out, sems = refs[len(entries) :]
    outs = (key_out, value_out)
    kv_width = key_out.shape[2]
    me = lax.axis_index("pool")
    total = jnp.int32(0)
    for other in range(pool_size):
        total += (owner_ref[other] == me).astype(jnp.int32)

    new_rows = key_out.shape[1]

    def copies(payload_ref, place):
        for i in range(2):
            for piece in range(new_rows // PIECE):
                row, lane = piece_place(i, piece, new_rows, kv_width)
                row += payload_ref.shape[0] - payload_rows(new_rows, kv_width)
                yield pltpu.make_async_copy(
                    payload_ref.at[row : row + PIECE, lane : lane + kv_width],
                    outs[i].at[place, piece * PIECE : (piece + 1) * PIECE],
                    sems.at[i, place, piece],
                )

    for entry, payload_ref in zip(entries, payload_refs):
        there, source = source_of(me, entry)
        rank = jnp.int32(0)
        for other in range(pool_size):
            rank += ((owner_ref[other] == me) & (other < source)).astype(jnp.int32)
        hit = there & (owner_ref[source] == me)
        for place in range(CAPP):

            @pl.when(hit & (rank == place))
            def _():
                for copy in copies(payload_ref, place):
                    copy.start()

    for place in range(CAPP):

        @pl.when(total <= place)
        def _():
            for out in outs:
                out[place] = jnp.zeros(out.shape[1:], jnp.bfloat16)

        @pl.when(total > place)
        def _():
            for copy in copies(payload_refs[0], place):
                copy.wait()


def combine_kernel(sources, last, own_ref, log_ref, *refs):
    parts = refs[: len(sources)]
    out_ref = refs[len(sources)]
    kv_width, rows = own_ref.shape
    me = lax.axis_index("pool")
    arrived = []
    tails = []
    for source, part in zip(sources, parts):
        there, request = source_of(me, source)
        arrived.append(there & (request != me))
        tails.append(part[kv_width:, :].astype(jnp.float32))
    if not last:
        refs[len(sources) + 1][...] = log_ref[...]
    for kv in range(kv_width // HD):
        logs = [log_ref[kv : kv + 1, :]]
        for there, tail in zip(arrived, tails):
            log = sum(tail[3 * kv + i : 3 * kv + i + 1] for i in range(3))
            logs.append(jnp.where(there, log, EMPTY))
        peak = functools.reduce(jnp.maximum, logs)
        shares = [jnp.exp(x - peak) for x in logs]
        total = functools.reduce(jnp.add, shares)
        shares = [x * (1.0 / total) for x in shares]
        band = slice(kv * HD, (kv + 1) * HD)
        for i in range(0, rows, TILE):
            part = slice(i, i + TILE)
            mixed = own_ref[band, part] * shares[0][:, part]
            for share, ref in zip(shares[1:], parts):
                mixed = mixed + ref[band, part].astype(jnp.float32) * share[:, part]
            if last:
                refs[len(sources) + 1][part, :] = mixed.astype(jnp.bfloat16).T
            else:
                out_ref[band, part] = mixed
        if last:
            turned = refs[len(sources) + 1]
            new_rows = out_ref.shape[0]
            for g in range(GROUP):
                head = kv * GROUP + g
                out_ref[:, head * HD : (head + 1) * HD] = turned[g * new_rows : (g + 1) * new_rows, :]
        else:
            refs[len(sources) + 1][kv : kv + 1, :] = peak + jnp.log(total)


def final_kernel(own_ref, log_ref, *refs):
    part_refs, (out_ref, buffer, turned, sems) = refs[:4], refs[4:]
    inner = is_inner(lax.axis_index("pool"))

    def copies(first):
        return [
            pltpu.make_async_copy(part_refs[first + i], buffer.at[i], sems.at[i]) for i in range(2)
        ]

    for hit, first in ((inner, 2), (jnp.logical_not(inner), 0)):

        @pl.when(hit)
        def _():
            for copy in copies(first):
                copy.start()

    for copy in copies(0):
        copy.wait()
    combine_kernel(
        [(1, 1), (2, 2)], True, own_ref, log_ref, buffer.at[0], buffer.at[1], out_ref, turned
    )


def shards(
    queries,
    new_keys,
    new_values,
    store_keys,
    store_values,
    prefix_blocks,
    hit_store,
    hit_slot,
    decode_owner,
):
    pool_size = lax.axis_size("pool")
    capacity = (MAXBLK + pool_size - 1) // pool_size
    new_rows = queries.shape[1]
    width = queries.shape[2]
    kv_width = new_keys.shape[2]
    block_len = store_keys.shape[1]
    rows = GROUP * new_rows
    tables = (prefix_blocks, hit_store, hit_slot)
    smem_spec = pl.BlockSpec(memory_space=pltpu.SMEM)
    hbm_spec = pl.BlockSpec(memory_space=pltpu.HBM)
    vmem_spec = pl.BlockSpec(memory_space=pltpu.VMEM)
    params = pltpu.CompilerParams(vmem_limit_bytes=VMEM_LIMIT)

    def cost(share):
        return pl.CostEstimate(
            flops=share * rows * block_len * kv_width * capacity,
            bytes_accessed=rows,
            transcendentals=0,
        )

    buffers = [pltpu.VMEM((capacity, block_len, kv_width), jnp.bfloat16)] * 2
    kv_local = kv_width // HD
    widest = block_len * min(2, capacity)
    work = [
        pltpu.VMEM((kv_local, widest, rows), jnp.float32),
        pltpu.VMEM((kv_local, widest, rows), jnp.bfloat16),
        pltpu.VMEM((kv_local, 8, rows), jnp.float32),
        pltpu.VMEM((kv_local, 8, rows), jnp.float32),
        pltpu.VMEM((kv_local, 8, rows), jnp.float32),
        pltpu.VMEM((kv_local, HD + ONES, widest), jnp.bfloat16),
        pltpu.VMEM((kv_local, HD + ONES, rows), jnp.float32),
    ]
    sems = pltpu.SemaphoreType.DMA((2, capacity))

    def own_part(payload):
        return pl.pallas_call(
            functools.partial(own_kernel, pool_size),
            in_specs=[smem_spec] * 3 + [vmem_spec] * 3 + [hbm_spec] * 2,
            out_specs=[vmem_spec] * 2,
            scratch_shapes=[
                *buffers,
                *[pltpu.VMEM((block_len, kv_width), jnp.bfloat16)] * 2,
                *work,
                sems,
            ],
            out_shape=[
                jax.ShapeDtypeStruct((kv_width, rows), jnp.float32),
                jax.ShapeDtypeStruct((8, rows), jnp.float32),
            ],
            compiler_params=params,
            cost_estimate=cost(8),
            name="own_part",
        )(*tables, payload, new_keys[0], new_values[0], store_keys, store_values)

    def other_part(partners, held, *request, share=8, moved=(), raw=False):
        if raw:
            out_shape = [
                jax.ShapeDtypeStruct((kv_local, HD + ONES, rows), jnp.float32),
                jax.ShapeDtypeStruct((kv_local, 8, rows), jnp.float32),
            ]
        else:
            out_shape = jax.ShapeDtypeStruct((kv_width + ONES, rows), jnp.bfloat16)
        more_specs = [hbm_spec] * 3 if moved else []
        return pl.pallas_call(
            functools.partial(other_kernel, pool_size, new_rows, partners, bool(moved), raw),
            in_specs=[smem_spec] * (3 + len(request))
            + [hbm_spec] * len(held)
            + more_specs
            + [hbm_spec] * 2,
            out_specs=[hbm_spec] * 2 if raw else hbm_spec,
            scratch_shapes=[
                *buffers,
                *work,
                pltpu.VMEM((kv_width, rows), jnp.bfloat16),
                pltpu.SemaphoreType.DMA,
                pltpu.VMEM((kv_width + ONES, rows), jnp.bfloat16),
                pltpu.SemaphoreType.DMA((max(2, kv_local + 1),)),
                sems,
            ],
            out_shape=out_shape,
            compiler_params=params,
            cost_estimate=cost(share),
            name="other_part",
        )(*request, *tables, *held, *moved, store_keys, store_values)

    def combine(own, log, sources, parts, last=True):
        if last:
            out_shape = jax.ShapeDtypeStruct((new_rows, width), jnp.bfloat16)
        else:
            out_shape = [
                jax.ShapeDtypeStruct((kv_width, rows), jnp.float32),
                jax.ShapeDtypeStruct((8, rows), jnp.float32),
            ]
        return pl.pallas_call(
            functools.partial(combine_kernel, tuple(sources), last),
            in_specs=[vmem_spec] * (2 + len(parts)),
            out_specs=vmem_spec if last else [vmem_spec] * 2,
            scratch_shapes=[pltpu.VMEM((rows, HD), jnp.bfloat16)] if last else [],
            out_shape=out_shape,
            compiler_params=params,
            cost_estimate=cost(0),
            name="combine",
        )(own, log, *parts)

    def final(own, log, parts):
        return pl.pallas_call(
            final_kernel,
            in_specs=[vmem_spec] * 2 + [hbm_spec] * 4,
            out_specs=vmem_spec,
            scratch_shapes=[
                pltpu.VMEM((2, kv_width + ONES, rows), jnp.bfloat16),
                pltpu.VMEM((rows, HD), jnp.bfloat16),
                pltpu.SemaphoreType.DMA((2,)),
            ],
            out_shape=jax.ShapeDtypeStruct((new_rows, width), jnp.bfloat16),
            compiler_params=params,
            name="final",
        )(own, log, *parts)

    payload = pl.pallas_call(
        prepare_kernel,
        in_specs=[vmem_spec] * 3,
        out_specs=vmem_spec,
        scratch_shapes=[pltpu.VMEM((rows, HD), jnp.bfloat16)],
        out_shape=jax.ShapeDtypeStruct((payload_rows(new_rows, kv_width), rows), jnp.bfloat16),
        compiler_params=params,
        name="prepare",
    )(queries[0], new_keys[0], new_values[0])
    own_out, own_log = own_part(payload)
    if pool_size == 4:
        def send(array, *pairs):
            return lax.ppermute(array, "pool", pairs)

        near = send(payload, (0, 1), (1, 0), (2, 3), (3, 2))
        middle = send(payload, (1, 2), (2, 1))
        blocks = pl.pallas_call(
            functools.partial(gather_kernel, pool_size),
            in_specs=[smem_spec] * 3 + [hbm_spec] * 2,
            out_specs=vmem_spec,
            scratch_shapes=[sems],
            out_shape=jax.ShapeDtypeStruct((2 * capacity, block_len, kv_width), jnp.bfloat16),
            compiler_params=params,
            name="gather_blocks",
        )(*tables, store_keys, store_values)
        blocks = send(blocks, (0, 1), (3, 2))
        near, middle, own_out, own_log = lax.optimization_barrier((near, middle, own_out, own_log))
        crossed = send(near, (1, 2), (2, 1))
        outward = send(middle, (1, 0), (2, 3))
        first = other_part((3, 1), (middle, near))
        across = send(first, (1, 2), (2, 1))
        near, first = lax.optimization_barrier((near, first))
        second = other_part((1, None), (near,))
        back = send(second, (1, 0), (2, 3))
        outward, second = lax.optimization_barrier((outward, second))
        outer_second = other_part((None, 2), (outward,))
        apart = send(outer_second, (0, 2), (3, 1))
        crossed, first, outer_second = lax.optimization_barrier((crossed, first, outer_second))
        inward = send(first, (0, 1), (3, 2))
        state = other_part((2, None), (crossed,), raw=True)
        crossed, state = lax.optimization_barrier((crossed, state))
        far = send(crossed[kv_width:], (1, 0), (2, 3))
        third = other_part((2, None), (crossed,), moved=(blocks, *state))
        ends = send(third, (1, 3), (2, 0))
        own_out, own_log, third = lax.optimization_barrier((own_out, own_log, third))
        own_out, own_log = combine(own_out, own_log, [(3, None)], [across], last=False)
        attended = final(own_out, own_log, (back, ends, apart, inward))
        moved = [
            ((0, 0), payload),
            ((1, 1), near),
            ((3, None), middle),
            ((2, None), crossed),
            ((None, 2), outward),
            ((None, 3), far),
        ]
    else:
        gathered = lax.all_gather(payload, "pool", axis=0, tiled=False)
        packed = lax.map(
            lambda pair: other_part(None, (pair[0],), pair[1].reshape(1)),
            (gathered, jnp.arange(pool_size, dtype=jnp.int32)),
        )
        parts = lax.all_to_all(packed, "pool", split_axis=0, concat_axis=0, tiled=True)
        attended = combine(own_out, own_log, list(range(pool_size)), parts)
        moved = [(source, gathered[source]) for source in range(pool_size)]

    pushed_keys, pushed_values = pl.pallas_call(
        functools.partial(push_kernel, pool_size, tuple(entry for entry, _ in moved)),
        in_specs=[smem_spec] + [hbm_spec] * len(moved),
        out_specs=[vmem_spec] * 2,
        scratch_shapes=[pltpu.SemaphoreType.DMA((2, CAPP, new_rows // PIECE))],
        out_shape=[jax.ShapeDtypeStruct((CAPP, new_rows, kv_width), jnp.bfloat16)] * 2,
        compiler_params=params,
        name="push",
    )(decode_owner, *[array for _, array in moved])
    return (attended[None], pushed_keys, pushed_values)


def solution(mesh):
    in_specs = (
        P(("groups", "pool"), None, ("tensor", "sub")),
        P(("groups", "pool"), None, ("tensor", "sub")),
        P(("groups", "pool"), None, ("tensor", "sub")),
        P(("groups", "pool"), None, ("tensor", "sub")),
        P(("groups", "pool"), None, ("tensor", "sub")),
        P("groups"),
        P("groups", None),
        P("groups", None),
        P("groups"),
    )
    out_specs = (
        P(("groups", "pool"), None, ("tensor", "sub")),
        P(("groups", "pool"), None, ("tensor", "sub")),
        P(("groups", "pool"), None, ("tensor", "sub")),
    )
    return jax.shard_map(shards, mesh=mesh, in_specs=in_specs, out_specs=out_specs, check_vma=False)
```

profile of v0, /device:TPU:0, one launch (start us, length us, event | category | flops | bytes accessed | tf_op | source)
XLA Modules:
  0.0 107.3 jit_solution(6970983326146251849)
XLA Ops:
  0.6 2.4 %prepare.1.payload_ref.refs_0_ = bf16[320,1280]{1,0:T(8,128)(2,1)} custom-call(bf16[160,2048]{1,0:T(8,128)(2,1)} %bitcast.4, bf16[160,256]{1,0:T(8,128)(2,1)} %bitcast.6, bf16[160,256]{1,0:T(8,128)(2,1)} %bitcast.8), custom_call_target="tpu_custom_call" | custom-call | tf_op jit(solution)/shard_map/prepare/pallas_call | solution.py:623
  3.0 3.0 %collective-permute-start = (bf16[320,1280]{1,0:T(8,128)(2,1)}, bf16[320,1280]{1,0:T(8,128)(2,1)}, u32[]{:S(2)}, u32[]{:S(2)}) collective-permute-start(bf16[320,1280]{1,0:T(8,128)(2,1)} %prepare.1.payload_ref.refs_0_), channel_id=1, source_target_pairs={{0,4},{4,0},{8,12},{12,8},{1,5},{5,1},{9,13},{13,9},{2,6},{6,2},{1... | collective-permute-start | bytes 2457608 | tf_op jit(solution)/shard_map/ppermute | solution.py:635
  6.0 1.7 %collective-permute-start.1 = (bf16[320,1280]{1,0:T(8,128)(2,1)}, bf16[320,1280]{1,0:T(8,128)(2,1)}, u32[]{:S(2)}, u32[]{:S(2)}) collective-permute-start(bf16[320,1280]{1,0:T(8,128)(2,1)} %prepare.1.payload_ref.refs_0_), channel_id=1, source_target_pairs={{4,8},{8,4},{5,9},{9,5},{6,10},{10,6},{7,11},{11,7},{20,24},{24,20... | collective-permute-start | bytes 2457608 | tf_op jit(solution)/shard_map/ppermute | solution.py:635
  7.7 3.6 %gather_blocks.1 = bf16[16,256,256]{2,1,0:T(8,128)(2,1)} custom-call(s32[4]{0:T(128)} %refs_0_.9, s32[4,32]{1,0:T(4,128)} %refs_1_.9, s32[4,32]{1,0:T(4,128)} %refs_2_.9, bf16[32,256,256]{2,1,0:T(8,128)(2,1)} %refs_7_.1, bf16[32,256,256]{2,1,0:T(8,128)(2,1)} %refs_8_.1), custom_call_target="tpu_custom_call" | custom-call | tf_op jit(solution)/shard_map/gather_blocks/pallas_call | solution.py:639
  11.3 5.3 %collective-permute-start.4 = (bf16[16,256,256]{2,1,0:T(8,128)(2,1)}, bf16[16,256,256]{2,1,0:T(8,128)(2,1)}, u32[]{:S(2)}, u32[]{:S(2)}) collective-permute-start(bf16[16,256,256]{2,1,0:T(8,128)(2,1)} %gather_blocks.1), channel_id=1, source_target_pairs={{0,4},{12,8},{1,5},{13,9},{2,6},{14,10},{3,7},{15,11},{16,20},{28,... | collective-permute-start | bytes 6291464 | tf_op jit(solution)/shard_map/ppermute | solution.py:635
  16.5 11.5 %own_part.1 = (f32[256,1280]{1,0:T(8,128)}, f32[8,1280]{1,0:T(8,128)}) custom-call(s32[4]{0:T(128)} %refs_0_.9, s32[4,32]{1,0:T(4,128)} %refs_1_.9, s32[4,32]{1,0:T(4,128)} %refs_2_.9, bf16[320,1280]{1,0:T(8,128)(2,1)} %prepare.1.payload_ref.refs_0_, bf16[160,256]{1,0:T(8,128)(2,1)} %bitcast.7, bf16[160,256]{1,0:T(8,128)(2,1)} %bitcast.9, ...), custom_call_target="tpu_custom_call" | custom-call | flops 5368709120 | bytes 1280 | tf_op jit(solution)/shard_map/own_part/pallas_call | solution.py:539
  28.1 0.0 collective-permute-done.1.refs_3_.refs_2_
  28.1 1.3 %collective-permute-start.3 = (bf16[320,1280]{1,0:T(8,128)(2,1)}, bf16[320,1280]{1,0:T(8,128)(2,1)}, u32[]{:S(2)}, u32[]{:S(2)}) collective-permute-start(bf16[320,1280]{1,0:T(8,128)(2,1)} %collective-permute-done.1.refs_3_.refs_2_), channel_id=1, source_target_pairs={{4,0},{8,12},{5,1},{9,13},{6,2},{10,14},{7,3},{11,15},{20,16},{24,... | collective-permute-start | bytes 2457608 | tf_op jit(solution)/shard_map/ppermute | solution.py:635
  29.4 1.6 %collective-permute-start.2 = (bf16[320,1280]{1,0:T(8,128)(2,1)}, bf16[320,1280]{1,0:T(8,128)(2,1)}, u32[]{:S(2)}, u32[]{:S(2)}) collective-permute-start(bf16[320,1280]{1,0:T(8,128)(2,1)} %collective-permute-done.refs_4_.refs_3_.refs_1_), channel_id=1, source_target_pairs={{4,8},{8,4},{5,9},{9,5},{6,10},{10,6},{7,11},{11,7},{20,24},{24,20... | collective-permute-start | bytes 2457608 | tf_op jit(solution)/shard_map/ppermute | solution.py:635
  31.0 7.9 %other_part.5 = bf16[272,1280]{1,0:T(8,128)(2,1)} custom-call(s32[4]{0:T(128)} %refs_0_.9, s32[4,32]{1,0:T(4,128)} %refs_1_.9, s32[4,32]{1,0:T(4,128)} %refs_2_.9, bf16[320,1280]{1,0:T(8,128)(2,1)} %collective-permute-done.1.refs_3_.refs_2_, bf16[320,1280]{1,0:T(8,128)(2,1)} %collective-permute-done.refs_4_.refs_3_.refs_1_, bf16[32,256,256]{2,1,0:T(8,128)(2,1)} %refs_7_.1, ...), custom_call_target="tpu_custom_call" | custom-call | flops 5368709120 | bytes 1280 | tf_op jit(solution)/shard_map/other_part/pallas_call | solution.py:567
  38.9 1.5 %collective-permute-start.5 = (bf16[272,1280]{1,0:T(8,128)(2,1)}, bf16[272,1280]{1,0:T(8,128)(2,1)}, u32[]{:S(2)}, u32[]{:S(2)}) collective-permute-start(bf16[272,1280]{1,0:T(8,128)(2,1)} %other_part.5), channel_id=1, source_target_pairs={{4,8},{8,4},{5,9},{9,5},{6,10},{10,6},{7,11},{11,7},{20,24},{24,20... | collective-permute-start | bytes 2088968 | tf_op jit(solution)/shard_map/ppermute | solution.py:635
  40.4 0.9 other_part.6
  41.4 1.3 %collective-permute-start.6 = (bf16[272,1280]{1,0:T(8,128)(2,1)}, bf16[272,1280]{1,0:T(8,128)(2,1)}, u32[]{:S(2)}, u32[]{:S(2)}) collective-permute-start(bf16[272,1280]{1,0:T(8,128)(2,1)} %other_part.6), channel_id=1, source_target_pairs={{4,0},{8,12},{5,1},{9,13},{6,2},{10,14},{7,3},{11,15},{20,16},{24,... | collective-permute-start | bytes 2088968 | tf_op jit(solution)/shard_map/ppermute | solution.py:635
  42.7 6.8 %collective-permute-done.3.refs_3_.refs_4_ = bf16[320,1280]{1,0:T(8,128)(2,1)} collective-permute-done((bf16[320,1280]{1,0:T(8,128)(2,1)}, bf16[320,1280]{1,0:T(8,128)(2,1)}, u32[]{:S(2)}, u32[]{:S(2)}) %collective-permute-start.3) | collective-permute-done | bytes 819232 | tf_op jit(solution)/shard_map/ppermute | solution.py:635
  49.4 10.7 %other_part.7 = bf16[272,1280]{1,0:T(8,128)(2,1)} custom-call(s32[4]{0:T(128)} %refs_0_.9, s32[4,32]{1,0:T(4,128)} %refs_1_.9, s32[4,32]{1,0:T(4,128)} %refs_2_.9, bf16[320,1280]{1,0:T(8,128)(2,1)} %collective-permute-done.3.refs_3_.refs_4_, bf16[32,256,256]{2,1,0:T(8,128)(2,1)} %refs_7_.1, bf16[32,256,256]{2,1,0:T(8,128)(2,1)} %refs_8_.1), custom_call_target="tpu_custom_call" | custom-call | flops 5368709120 | bytes 1280 | tf_op jit(solution)/shard_map/other_part/pallas_call | solution.py:567
  60.2 3.8 %collective-permute-start.8 = (bf16[272,1280]{1,0:T(8,128)(2,1)}, bf16[272,1280]{1,0:T(8,128)(2,1)}, u32[]{:S(2)}, u32[]{:S(2)}) collective-permute-start(bf16[272,1280]{1,0:T(8,128)(2,1)} %other_part.7), channel_id=1, source_target_pairs={{0,8},{12,4},{1,9},{13,5},{2,10},{14,6},{3,11},{15,7},{16,24},{28,... | collective-permute-start | bytes 2088968 | tf_op jit(solution)/shard_map/ppermute | solution.py:635
  63.9 0.0 collective-permute-done.2.refs_3_
  63.9 0.9 other_part.8
  64.9 0.9 slice.3
  65.8 1.3 %collective-permute-start.10 = (bf16[64,1280]{1,0:T(8,128)(2,1)S(1)}, bf16[64,1280]{1,0:T(8,128)(2,1)S(1)}, u32[]{:S(2)}, u32[]{:S(2)}) collective-permute-start(bf16[64,1280]{1,0:T(8,128)(2,1)S(1)} %slice.3), channel_id=1, source_target_pairs={{4,0},{8,12},{5,1},{9,13},{6,2},{10,14},{7,3},{11,15},{20,16},{24,... | collective-permute-start | bytes 491528 | tf_op jit(solution)/shard_map/ppermute | solution.py:635
  67.1 2.8 %collective-permute-done.4.refs_4_ = bf16[16,256,256]{2,1,0:T(8,128)(2,1)} collective-permute-done((bf16[16,256,256]{2,1,0:T(8,128)(2,1)}, bf16[16,256,256]{2,1,0:T(8,128)(2,1)}, u32[]{:S(2)}, u32[]{:S(2)}) %collective-permute-start.4) | collective-permute-done | bytes 2097184 | tf_op jit(solution)/shard_map/ppermute | solution.py:635
  69.9 6.2 %collective-permute-start.9 = (bf16[272,1280]{1,0:T(8,128)(2,1)}, bf16[272,1280]{1,0:T(8,128)(2,1)}, u32[]{:S(2)}, u32[]{:S(2)}) collective-permute-start(bf16[272,1280]{1,0:T(8,128)(2,1)} %other_part.5), channel_id=1, source_target_pairs={{0,4},{12,8},{1,5},{13,9},{2,6},{14,10},{3,7},{15,11},{16,20},{28,... | collective-permute-start | bytes 2088968 | tf_op jit(solution)/shard_map/ppermute | solution.py:635
  76.1 0.9 other_part.9
  77.0 0.4 collective-permute-done.10.refs_5_
  77.4 1.3 %collective-permute-start.7 = (bf16[272,1280]{1,0:T(8,128)(2,1)}, bf16[272,1280]{1,0:T(8,128)(2,1)}, u32[]{:S(2)}, u32[]{:S(2)}) collective-permute-start(bf16[272,1280]{1,0:T(8,128)(2,1)} %other_part.9), channel_id=1, source_target_pairs={{4,12},{8,0},{5,13},{9,1},{6,14},{10,2},{7,15},{11,3},{20,28},{24,... | collective-permute-start | bytes 2088968 | tf_op jit(solution)/shard_map/ppermute | solution.py:635
  78.7 2.5 %push.1 = (bf16[2,160,256]{2,1,0:T(8,128)(2,1)}, bf16[2,160,256]{2,1,0:T(8,128)(2,1)}) custom-call(s32[4]{0:T(128)} %owner_ref.1, bf16[320,1280]{1,0:T(8,128)(2,1)} %prepare.1.payload_ref.refs_0_, bf16[320,1280]{1,0:T(8,128)(2,1)} %collective-permute-done.refs_4_.refs_3_.refs_1_, bf16[320,1280]{1,0:T(8,128)(2,1)} %collective-permute-done.1.refs_3_.refs_2_, ...), custom_call_target="tpu_custom_call" | custom-call | tf_op jit(solution)/shard_map/push/pallas_call | solution.py:688
  81.2 0.0 collective-permute-done.5.refs_0_
  81.2 2.9 %combine.1 = (f32[256,1280]{1,0:T(8,128)}, f32[8,1280]{1,0:T(8,128)}) custom-call(f32[256,1280]{1,0:T(8,128)} %get-tuple-element.40.own_ref, f32[8,1280]{1,0:T(8,128)} %get-tuple-element.41.log_ref, bf16[272,1280]{1,0:T(8,128)(2,1)} %collective-permute-done.5.refs_0_), custom_call_target="tpu_custom_call" | custom-call | bytes 1280 | tf_op jit(solution)/shard_map/combine/pallas_call | solution.py:597
  84.1 0.0 collective-permute-done.6.refs_0_
  84.1 14.5 %collective-permute-done.9.refs_3_ = bf16[272,1280]{1,0:T(8,128)(2,1)} collective-permute-done((bf16[272,1280]{1,0:T(8,128)(2,1)}, bf16[272,1280]{1,0:T(8,128)(2,1)}, u32[]{:S(2)}, u32[]{:S(2)}) %collective-permute-start.9) | collective-permute-done | bytes 696352 | tf_op jit(solution)/shard_map/ppermute | solution.py:635
  98.6 4.5 %collective-permute-done.7.refs_1_ = bf16[272,1280]{1,0:T(8,128)(2,1)} collective-permute-done((bf16[272,1280]{1,0:T(8,128)(2,1)}, bf16[272,1280]{1,0:T(8,128)(2,1)}, u32[]{:S(2)}, u32[]{:S(2)}) %collective-permute-start.7) | collective-permute-done | bytes 696352 | tf_op jit(solution)/shard_map/ppermute | solution.py:635
  103.1 4.1 %final.1 = bf16[160,2048]{1,0:T(8,128)(2,1)} custom-call(f32[256,1280]{1,0:T(8,128)} %get-tuple-element.42.own_ref, f32[8,1280]{1,0:T(8,128)} %get-tuple-element.43.log_ref, bf16[272,1280]{1,0:T(8,128)(2,1)} %collective-permute-done.6.refs_0_, bf16[272,1280]{1,0:T(8,128)(2,1)} %collective-permute-done.7.refs_1_, ...), custom_call_target="tpu_custom_call" | custom-call | tf_op jit(solution)/shard_map/final/pallas_call | solution.py:609
  (4 shorter events, 0.0 us)
Async XLA Ops:
  3.0 25.1 %collective-permute-start = (bf16[320,1280]{1,0:T(8,128)(2,1)}, bf16[320,1280]{1,0:T(8,128)(2,1)}, u32[]{:S(2)}, u32[]{:S(2)}) collective-permute-start(bf16[320,1280]{1,0:T(8,128)(2,1)} %prepare.1.payload_ref.refs_0_), channel_id=1, source_target_pairs={{0,4},{4,0},{8,12},{12,8},{1,5},{5,1},{9,13},{13,9},{2,6},{6,2},{1... | collective-permute-start | bytes 2457608 | tf_op jit(solution)/shard_map/ppermute | solution.py:635
  6.0 22.1 %collective-permute-start.1 = (bf16[320,1280]{1,0:T(8,128)(2,1)}, bf16[320,1280]{1,0:T(8,128)(2,1)}, u32[]{:S(2)}, u32[]{:S(2)}) collective-permute-start(bf16[320,1280]{1,0:T(8,128)(2,1)} %prepare.1.payload_ref.refs_0_), channel_id=1, source_target_pairs={{4,8},{8,4},{5,9},{9,5},{6,10},{10,6},{7,11},{11,7},{20,24},{24,20... | collective-permute-start | bytes 2457608 | tf_op jit(solution)/shard_map/ppermute | solution.py:635
  11.3 58.7 %collective-permute-start.4 = (bf16[16,256,256]{2,1,0:T(8,128)(2,1)}, bf16[16,256,256]{2,1,0:T(8,128)(2,1)}, u32[]{:S(2)}, u32[]{:S(2)}) collective-permute-start(bf16[16,256,256]{2,1,0:T(8,128)(2,1)} %gather_blocks.1), channel_id=1, source_target_pairs={{0,4},{12,8},{1,5},{13,9},{2,6},{14,10},{3,7},{15,11},{16,20},{28,... | collective-permute-start | bytes 6291464 | tf_op jit(solution)/shard_map/ppermute | solution.py:635
  28.1 21.4 %collective-permute-start.3 = (bf16[320,1280]{1,0:T(8,128)(2,1)}, bf16[320,1280]{1,0:T(8,128)(2,1)}, u32[]{:S(2)}, u32[]{:S(2)}) collective-permute-start(bf16[320,1280]{1,0:T(8,128)(2,1)} %collective-permute-done.1.refs_3_.refs_2_), channel_id=1, source_target_pairs={{4,0},{8,12},{5,1},{9,13},{6,2},{10,14},{7,3},{11,15},{20,16},{24,... | collective-permute-start | bytes 2457608 | tf_op jit(solution)/shard_map/ppermute | solution.py:635
  29.4 34.6 %collective-permute-start.2 = (bf16[320,1280]{1,0:T(8,128)(2,1)}, bf16[320,1280]{1,0:T(8,128)(2,1)}, u32[]{:S(2)}, u32[]{:S(2)}) collective-permute-start(bf16[320,1280]{1,0:T(8,128)(2,1)} %collective-permute-done.refs_4_.refs_3_.refs_1_), channel_id=1, source_target_pairs={{4,8},{8,4},{5,9},{9,5},{6,10},{10,6},{7,11},{11,7},{20,24},{24,20... | collective-permute-start | bytes 2457608 | tf_op jit(solution)/shard_map/ppermute | solution.py:635
  38.9 42.3 %collective-permute-start.5 = (bf16[272,1280]{1,0:T(8,128)(2,1)}, bf16[272,1280]{1,0:T(8,128)(2,1)}, u32[]{:S(2)}, u32[]{:S(2)}) collective-permute-start(bf16[272,1280]{1,0:T(8,128)(2,1)} %other_part.5), channel_id=1, source_target_pairs={{4,8},{8,4},{5,9},{9,5},{6,10},{10,6},{7,11},{11,7},{20,24},{24,20... | collective-permute-start | bytes 2088968 | tf_op jit(solution)/shard_map/ppermute | solution.py:635
  41.4 42.8 %collective-permute-start.6 = (bf16[272,1280]{1,0:T(8,128)(2,1)}, bf16[272,1280]{1,0:T(8,128)(2,1)}, u32[]{:S(2)}, u32[]{:S(2)}) collective-permute-start(bf16[272,1280]{1,0:T(8,128)(2,1)} %other_part.6), channel_id=1, source_target_pairs={{4,0},{8,12},{5,1},{9,13},{6,2},{10,14},{7,3},{11,15},{20,16},{24,... | collective-permute-start | bytes 2088968 | tf_op jit(solution)/shard_map/ppermute | solution.py:635
  60.2 38.4 %collective-permute-start.8 = (bf16[272,1280]{1,0:T(8,128)(2,1)}, bf16[272,1280]{1,0:T(8,128)(2,1)}, u32[]{:S(2)}, u32[]{:S(2)}) collective-permute-start(bf16[272,1280]{1,0:T(8,128)(2,1)} %other_part.7), channel_id=1, source_target_pairs={{0,8},{12,4},{1,9},{13,5},{2,10},{14,6},{3,11},{15,7},{16,24},{28,... | collective-permute-start | bytes 2088968 | tf_op jit(solution)/shard_map/ppermute | solution.py:635
  65.8 11.6 %collective-permute-start.10 = (bf16[64,1280]{1,0:T(8,128)(2,1)S(1)}, bf16[64,1280]{1,0:T(8,128)(2,1)S(1)}, u32[]{:S(2)}, u32[]{:S(2)}) collective-permute-start(bf16[64,1280]{1,0:T(8,128)(2,1)S(1)} %slice.3), channel_id=1, source_target_pairs={{4,0},{8,12},{5,1},{9,13},{6,2},{10,14},{7,3},{11,15},{20,16},{24,... | collective-permute-start | bytes 491528 | tf_op jit(solution)/shard_map/ppermute | solution.py:635
  69.9 28.7 %collective-permute-start.9 = (bf16[272,1280]{1,0:T(8,128)(2,1)}, bf16[272,1280]{1,0:T(8,128)(2,1)}, u32[]{:S(2)}, u32[]{:S(2)}) collective-permute-start(bf16[272,1280]{1,0:T(8,128)(2,1)} %other_part.5), channel_id=1, source_target_pairs={{0,4},{12,8},{1,5},{13,9},{2,6},{14,10},{3,7},{15,11},{16,20},{28,... | collective-permute-start | bytes 2088968 | tf_op jit(solution)/shard_map/ppermute | solution.py:635
  77.4 1.3 %copy-start = (bf16[64,1280]{1,0:T(8,128)(2,1)}, bf16[64,1280]{1,0:T(8,128)(2,1)S(1)}, u32[]{:S(2)}) copy-start(bf16[64,1280]{1,0:T(8,128)(2,1)S(1)} %collective-permute-done.10.refs_5_) | copy-start | bytes 491524
  77.4 25.7 %collective-permute-start.7 = (bf16[272,1280]{1,0:T(8,128)(2,1)}, bf16[272,1280]{1,0:T(8,128)(2,1)}, u32[]{:S(2)}, u32[]{:S(2)}) collective-permute-start(bf16[272,1280]{1,0:T(8,128)(2,1)} %other_part.9), channel_id=1, source_target_pairs={{4,12},{8,0},{5,13},{9,1},{6,14},{10,2},{7,15},{11,3},{20,28},{24,... | collective-permute-start | bytes 2088968 | tf_op jit(solution)/shard_map/ppermute | solution.py:635
where the time goes:
time: 107 us
  Pallas kernels  48.3 us (45%)
  waiting for transfers between devices  29 us (27%)
  starting transfers between devices  28.1 us (26%)
    ppermute x11, waiting for transfers between devices, send(): return lax.ppermute(array, 'pool', pairs)  29 us
    ppermute x11, starting transfers between devices, send(): return lax.ppermute(array, 'pool', pairs)  28.1 us
    pallas_call x5, Pallas kernels, other_part(): pl.pallas_call(functools.partial(other_kernel, pool_size, new_rows, partn...  21.5 us
    pallas_call x1, Pallas kernels, own_part(): pl.pallas_call(functools.partial(own_kernel, pool_size), in_specs=[smem_s...  11.5 us
    pallas_call x1, Pallas kernels, final(): pl.pallas_call(final_kernel, in_specs=[vmem_spec] * 2 + [hbm_spec] * 4, o...  4.05 us
    pallas_call x1, Pallas kernels, shards(): pl.pallas_call(functools.partial(gather_kernel, pool_size), in_specs=[sme...  3.59 us
    pallas_call x1, Pallas kernels, combine(): pl.pallas_call(functools.partial(combine_kernel, tuple(sources), last), i...  2.87 us
    pallas_call x1, Pallas kernels, shards(): pl.pallas_call(functools.partial(push_kernel, pool_size, tuple((entry for...  2.51 us
  transfers between devices with their start and end apart: 11, of which 5 were waited for; matrix products, arithmetic and copies ran while one was open for 1% of the time, Pallas kernels for 39%

commit v1 on v0

--- a/solution.py
+++ b/solution.py
@@ -284,7 +284,7 @@
         moved, *initial = refs[:3]
         refs = refs[3:]
     store_keys, store_values, *refs = refs
-    results_ref, (key_buf, value_buf, *state) = refs[: 1 + raw], refs[1 + raw :]
+    results_ref, (key_buf, value_buf, *state) = refs[: 1 + 2 * raw], refs[1 + 2 * raw :]
     *work, columns, query_sem, out_buf, out_sem, sems = state
     kv_width = columns.shape[0]
 
@@ -306,6 +306,11 @@
             sems,
             moved,
         )
+        if raw:
+            passed = pltpu.make_async_copy(
+                payload_refs[0].at[kv_width:], results_ref[2], out_sem.at[2]
+            )
+            passed.start()
         restore = None
         if initial is not None:
 
@@ -328,7 +333,7 @@
             ]
             for copy in copies:
                 copy.start()
-            for copy in copies:
+            for copy in (*copies, passed):
                 copy.wait()
             return
         outs, logs = results
@@ -467,27 +472,60 @@
             refs[len(sources) + 1][kv : kv + 1, :] = peak + jnp.log(total)
 
 
-def final_kernel(own_ref, log_ref, *refs):
-    part_refs, (out_ref, buffer, turned, sems) = refs[:4], refs[4:]
+def final_kernel(own_ref, log_ref, outer_ref, inner_ref, out_ref, own_buf, part_buf, out_buf, turned, sems):
+    kv_width, rows = own_buf.shape
+    new_rows = out_buf.shape[0]
+    kv_local = kv_width // HD
+    lanes = GROUP * HD
     inner = is_inner(lax.axis_index("pool"))
-
-    def copies(first):
+    bands = [slice(kv * HD, (kv + 1) * HD) for kv in range(kv_local)] + [slice(kv_width, kv_width + ONES)]
+
+    def part_copies(ref):
         return [
-            pltpu.make_async_copy(part_refs[first + i], buffer.at[i], sems.at[i]) for i in range(2)
+            pltpu.make_async_copy(ref.at[band], part_buf.at[band], sems.at[0, i])
+            for i, band in enumerate(bands)
         ]
 
-    for hit, first in ((inner, 2), (jnp.logical_not(inner), 0)):
-
-        @pl.when(hit)
-        def _():
-            for copy in copies(first):
-                copy.start()
-
-    for copy in copies(0):
+    def start_part(ref):
+        for copy in reversed(part_copies(ref)):
+            copy.start()
+
+    own_copies = [
+        pltpu.make_async_copy(own_ref.at[band], own_buf.at[band], sems.at[1, i])
+        for i, band in enumerate(bands[:-1])
+    ]
+    pl.when(inner)(functools.partial(start_part, inner_ref))
+    pl.when(jnp.logical_not(inner))(functools.partial(start_part, outer_ref))
+    for copy in own_copies:
+        copy.start()
+    arriving = part_copies(outer_ref)
+    arriving[-1].wait()
+    tail = part_buf[kv_width:, :].astype(jnp.float32)
+    leaving = []
+    for kv in range(kv_local):
+        log = log_ref[kv : kv + 1, :]
+        other = sum(tail[3 * kv + i : 3 * kv + i + 1] for i in range(3))
+        peak = jnp.maximum(log, other)
+        shares = [jnp.exp(log - peak), jnp.exp(other - peak)]
+        scale = 1.0 / (shares[0] + shares[1])
+        shares = [share * scale for share in shares]
+        arriving[kv].wait()
+        own_copies[kv].wait()
+        for i in range(0, rows, TILE):
+            part = slice(i, i + TILE)
+            mixed = own_buf[bands[kv], part] * shares[0][:, part]
+            mixed = mixed + part_buf[bands[kv], part].astype(jnp.float32) * shares[1][:, part]
+            turned[part, :] = mixed.astype(jnp.bfloat16).T
+        for g in range(GROUP):
+            head = kv * GROUP + g
+            out_buf[:, head * HD : (head + 1) * HD] = turned[g * new_rows : (g + 1) * new_rows, :]
+        band = slice(kv * lanes, (kv + 1) * lanes)
+        leaving.append(
+            pltpu.make_async_copy(out_buf.at[:, band], out_ref.at[:, band], sems.at[2, kv])
+        )
+        leaving[-1].start()
+    for copy in leaving:
         copy.wait()
-    combine_kernel(
-        [(1, 1), (2, 2)], True, own_ref, log_ref, buffer.at[0], buffer.at[1], out_ref, turned
-    )
 
 
 def shards(
@@ -560,6 +598,7 @@
             out_shape = [
                 jax.ShapeDtypeStruct((kv_local, HD + ONES, rows), jnp.float32),
                 jax.ShapeDtypeStruct((kv_local, 8, rows), jnp.float32),
+                jax.ShapeDtypeStruct((held[0].shape[0] - kv_width, rows), jnp.bfloat16),
             ]
         else:
             out_shape = jax.ShapeDtypeStruct((kv_width + ONES, rows), jnp.bfloat16)
@@ -570,14 +609,14 @@
             + [hbm_spec] * len(held)
             + more_specs
             + [hbm_spec] * 2,
-            out_specs=[hbm_spec] * 2 if raw else hbm_spec,
+            out_specs=[hbm_spec] * 3 if raw else hbm_spec,
             scratch_shapes=[
                 *buffers,
                 *work,
                 pltpu.VMEM((kv_width, rows), jnp.bfloat16),
                 pltpu.SemaphoreType.DMA,
                 pltpu.VMEM((kv_width + ONES, rows), jnp.bfloat16),
-                pltpu.SemaphoreType.DMA((max(2, kv_local + 1),)),
+                pltpu.SemaphoreType.DMA((max(3, kv_local + 1),)),
                 sems,
             ],
             out_shape=out_shape,
@@ -608,12 +647,14 @@
     def final(own, log, parts):
         return pl.pallas_call(
             final_kernel,
-            in_specs=[vmem_spec] * 2 + [hbm_spec] * 4,
-            out_specs=vmem_spec,
+            in_specs=[hbm_spec, vmem_spec, hbm_spec, hbm_spec],
+            out_specs=hbm_spec,
             scratch_shapes=[
-                pltpu.VMEM((2, kv_width + ONES, rows), jnp.bfloat16),
+                pltpu.VMEM((kv_width, rows), jnp.float32),
+                pltpu.VMEM((kv_width + ONES, rows), jnp.bfloat16),
+                pltpu.VMEM((new_rows, width), jnp.bfloat16),
                 pltpu.VMEM((rows, HD), jnp.bfloat16),
-                pltpu.SemaphoreType.DMA((2,)),
+                pltpu.SemaphoreType.DMA((3, kv_local + 1)),
             ],
             out_shape=jax.ShapeDtypeStruct((new_rows, width), jnp.bfloat16),
             compiler_params=params,
@@ -650,23 +691,26 @@
         crossed = send(near, (1, 2), (2, 1))
         outward = send(middle, (1, 0), (2, 3))
         first = other_part((3, 1), (middle, near))
-        across = send(first, (1, 2), (2, 1))
         near, first = lax.optimization_barrier((near, first))
         second = other_part((1, None), (near,))
+        first, second = lax.optimization_barrier((first, second))
+        across = send(first, (1, 2), (2, 1))
         back = send(second, (1, 0), (2, 3))
         outward, second = lax.optimization_barrier((outward, second))
         outer_second = other_part((None, 2), (outward,))
         apart = send(outer_second, (0, 2), (3, 1))
         crossed, first, outer_second = lax.optimization_barrier((crossed, first, outer_second))
         inward = send(first, (0, 1), (3, 2))
-        state = other_part((2, None), (crossed,), raw=True)
+        *state, fresh = other_part((2, None), (crossed,), raw=True)
         crossed, state = lax.optimization_barrier((crossed, state))
-        far = send(crossed[kv_width:], (1, 0), (2, 3))
+        far = send(fresh, (1, 0), (2, 3))
         third = other_part((2, None), (crossed,), moved=(blocks, *state))
         ends = send(third, (1, 3), (2, 0))
         own_out, own_log, third = lax.optimization_barrier((own_out, own_log, third))
-        own_out, own_log = combine(own_out, own_log, [(3, None)], [across], last=False)
-        attended = final(own_out, own_log, (back, ends, apart, inward))
+        own_out, own_log = combine(
+            own_out, own_log, [(3, None), (2, None), (None, 1)], [across, apart, back], last=False
+        )
+        attended = final(own_out, own_log, (ends, inward))
         moved = [
             ((0, 0), payload),
             ((1, 1), near),

time: 107 us -> 107 us (level)
  waiting for transfers between devices: 29 us -> 24.5 us
  starting transfers between devices: 28.1 us -> 31.7 us
  Pallas kernels: 48.3 us -> 50.5 us
    ppermute x11, waiting for transfers between devices: 29 us -> 24.5 us  [send(): return lax.ppermute(array, 'pool', pairs)]
    ppermute x11, starting transfers between devices: 28.1 us -> 31.7 us  [send(): return lax.ppermute(array, 'pool', pairs)]
    pallas_call x5, Pallas kernels: 21.5 us -> 24.1 us  [other_part(): pl.pallas_call(functools.partial(other_kernel, pool_size, new_rows, partn...]
  transfers between devices with their start and end apart: 11 -> 11, of which waited for: 5 -> 5; matrix products, arithmetic and copies ran while one was open for 1% -> 0% of each run, Pallas kernels for 39% -> 42%
where the time goes in v1:
time: 107 us; the launch traced here: 108 us
  Pallas kernels  50.5 us (47%)
  starting transfers between devices  31.7 us (30%)
  waiting for transfers between devices  24.5 us (23%)
    ppermute x11, starting transfers between devices, send(): return lax.ppermute(array, 'pool', pairs)  31.7 us
    ppermute x11, waiting for transfers between devices, send(): return lax.ppermute(array, 'pool', pairs)  24.5 us
    pallas_call x5, Pallas kernels, other_part(): pl.pallas_call(functools.partial(other_kernel, pool_size, new_rows, partn...  24.1 us
    pallas_call x1, Pallas kernels, own_part(): pl.pallas_call(functools.partial(own_kernel, pool_size), in_specs=[smem_s...  10.8 us
    pallas_call x1, Pallas kernels, shards(): pl.pallas_call(functools.partial(gather_kernel, pool_size), in_specs=[sme...  3.83 us
    pallas_call x1, Pallas kernels, combine(): pl.pallas_call(functools.partial(combine_kernel, tuple(sources), last), i...  3.61 us
    pallas_call x1, Pallas kernels, final(): pl.pallas_call(final_kernel, in_specs=[hbm_spec, vmem_spec, hbm_spec, hbm...  3.33 us
    pallas_call x1, Pallas kernels, shards(): pl.pallas_call(functools.partial(push_kernel, pool_size, tuple((entry for...  2.51 us
  transfers between devices with their start and end apart: 11, of which 5 were waited for; matrix products, arithmetic and copies ran while one was open for 0% of the time, Pallas kernels for 42%

profile of v1, /device:TPU:0, one launch (start us, length us, event | category | flops | bytes accessed | tf_op | source)
XLA Modules:
  0.0 107.7 jit_solution(368291036836423420)
XLA Ops:
  0.6 2.4 %prepare.1.payload_ref.refs_0_ = bf16[320,1280]{1,0:T(8,128)(2,1)} custom-call(bf16[160,2048]{1,0:T(8,128)(2,1)} %bitcast.4, bf16[160,256]{1,0:T(8,128)(2,1)} %bitcast.6, bf16[160,256]{1,0:T(8,128)(2,1)} %bitcast.8), custom_call_target="tpu_custom_call" | custom-call | tf_op jit(solution)/shard_map/prepare/pallas_call | solution.py:664
  3.0 3.0 %collective-permute-start = (bf16[320,1280]{1,0:T(8,128)(2,1)}, bf16[320,1280]{1,0:T(8,128)(2,1)}, u32[]{:S(2)}, u32[]{:S(2)}) collective-permute-start(bf16[320,1280]{1,0:T(8,128)(2,1)} %prepare.1.payload_ref.refs_0_), channel_id=1, source_target_pairs={{0,4},{4,0},{8,12},{12,8},{1,5},{5,1},{9,13},{13,9},{2,6},{6,2},{1... | collective-permute-start | bytes 2457608 | tf_op jit(solution)/shard_map/ppermute | solution.py:676
  6.0 1.7 %collective-permute-start.1 = (bf16[320,1280]{1,0:T(8,128)(2,1)}, bf16[320,1280]{1,0:T(8,128)(2,1)}, u32[]{:S(2)}, u32[]{:S(2)}) collective-permute-start(bf16[320,1280]{1,0:T(8,128)(2,1)} %prepare.1.payload_ref.refs_0_), channel_id=1, source_target_pairs={{4,8},{8,4},{5,9},{9,5},{6,10},{10,6},{7,11},{11,7},{20,24},{24,20... | collective-permute-start | bytes 2457608 | tf_op jit(solution)/shard_map/ppermute | solution.py:676
  7.7 3.8 %gather_blocks.1 = bf16[16,256,256]{2,1,0:T(8,128)(2,1)} custom-call(s32[4]{0:T(128)} %refs_0_.9, s32[4,32]{1,0:T(4,128)} %refs_1_.9, s32[4,32]{1,0:T(4,128)} %refs_2_.9, bf16[32,256,256]{2,1,0:T(8,128)(2,1)} %refs_7_.1, bf16[32,256,256]{2,1,0:T(8,128)(2,1)} %refs_8_.1), custom_call_target="tpu_custom_call" | custom-call | tf_op jit(solution)/shard_map/gather_blocks/pallas_call | solution.py:680
  11.5 5.0 %collective-permute-start.4 = (bf16[16,256,256]{2,1,0:T(8,128)(2,1)}, bf16[16,256,256]{2,1,0:T(8,128)(2,1)}, u32[]{:S(2)}, u32[]{:S(2)}) collective-permute-start(bf16[16,256,256]{2,1,0:T(8,128)(2,1)} %gather_blocks.1), channel_id=1, source_target_pairs={{0,4},{12,8},{1,5},{13,9},{2,6},{14,10},{3,7},{15,11},{16,20},{28,... | collective-permute-start | bytes 6291464 | tf_op jit(solution)/shard_map/ppermute | solution.py:676
  16.5 10.8 %own_part.1 = (f32[256,1280]{1,0:T(8,128)}, f32[8,1280]{1,0:T(8,128)}) custom-call(s32[4]{0:T(128)} %refs_0_.9, s32[4,32]{1,0:T(4,128)} %refs_1_.9, s32[4,32]{1,0:T(4,128)} %refs_2_.9, bf16[320,1280]{1,0:T(8,128)(2,1)} %prepare.1.payload_ref.refs_0_, bf16[160,256]{1,0:T(8,128)(2,1)} %bitcast.7, bf16[160,256]{1,0:T(8,128)(2,1)} %bitcast.9, ...), custom_call_target="tpu_custom_call" | custom-call | flops 5368709120 | bytes 1280 | tf_op jit(solution)/shard_map/own_part/pallas_call | solution.py:577
  27.3 0.0 collective-permute-done.refs_4_.refs_3_.refs_1_
  27.3 0.0 collective-permute-done.1.refs_3_.refs_2_
  27.3 1.3 %collective-permute-start.3 = (bf16[320,1280]{1,0:T(8,128)(2,1)}, bf16[320,1280]{1,0:T(8,128)(2,1)}, u32[]{:S(2)}, u32[]{:S(2)}) collective-permute-start(bf16[320,1280]{1,0:T(8,128)(2,1)} %collective-permute-done.1.refs_3_.refs_2_), channel_id=1, source_target_pairs={{4,0},{8,12},{5,1},{9,13},{6,2},{10,14},{7,3},{11,15},{20,16},{24,... | collective-permute-start | bytes 2457608 | tf_op jit(solution)/shard_map/ppermute | solution.py:676
  28.6 1.6 %collective-permute-start.2 = (bf16[320,1280]{1,0:T(8,128)(2,1)}, bf16[320,1280]{1,0:T(8,128)(2,1)}, u32[]{:S(2)}, u32[]{:S(2)}) collective-permute-start(bf16[320,1280]{1,0:T(8,128)(2,1)} %collective-permute-done.refs_4_.refs_3_.refs_1_), channel_id=1, source_target_pairs={{4,8},{8,4},{5,9},{9,5},{6,10},{10,6},{7,11},{11,7},{20,24},{24,20... | collective-permute-start | bytes 2457608 | tf_op jit(solution)/shard_map/ppermute | solution.py:676
  30.2 10.6 %other_part.5 = bf16[272,1280]{1,0:T(8,128)(2,1)} custom-call(s32[4]{0:T(128)} %refs_0_.9, s32[4,32]{1,0:T(4,128)} %refs_1_.9, s32[4,32]{1,0:T(4,128)} %refs_2_.9, bf16[320,1280]{1,0:T(8,128)(2,1)} %collective-permute-done.1.refs_3_.refs_2_, bf16[320,1280]{1,0:T(8,128)(2,1)} %collective-permute-done.refs_4_.refs_3_.refs_1_, bf16[32,256,256]{2,1,0:T(8,128)(2,1)} %refs_7_.1, ...), custom_call_target="tpu_custom_call" | custom-call | flops 5368709120 | bytes 1280 | tf_op jit(solution)/shard_map/other_part/pallas_call | solution.py:606
  40.8 0.9 other_part.6
  41.7 1.6 %collective-permute-start.5 = (bf16[272,1280]{1,0:T(8,128)(2,1)}, bf16[272,1280]{1,0:T(8,128)(2,1)}, u32[]{:S(2)}, u32[]{:S(2)}) collective-permute-start(bf16[272,1280]{1,0:T(8,128)(2,1)} %other_part.5), channel_id=1, source_target_pairs={{4,8},{8,4},{5,9},{9,5},{6,10},{10,6},{7,11},{11,7},{20,24},{24,20... | collective-permute-start | bytes 2088968 | tf_op jit(solution)/shard_map/ppermute | solution.py:676
  43.3 1.3 %collective-permute-start.7 = (bf16[272,1280]{1,0:T(8,128)(2,1)}, bf16[272,1280]{1,0:T(8,128)(2,1)}, u32[]{:S(2)}, u32[]{:S(2)}) collective-permute-start(bf16[272,1280]{1,0:T(8,128)(2,1)} %other_part.6), channel_id=1, source_target_pairs={{4,0},{8,12},{5,1},{9,13},{6,2},{10,14},{7,3},{11,15},{20,16},{24,... | collective-permute-start | bytes 2088968 | tf_op jit(solution)/shard_map/ppermute | solution.py:676
  44.6 4.1 %collective-permute-done.3.refs_3_.refs_4_ = bf16[320,1280]{1,0:T(8,128)(2,1)} collective-permute-done((bf16[320,1280]{1,0:T(8,128)(2,1)}, bf16[320,1280]{1,0:T(8,128)(2,1)}, u32[]{:S(2)}, u32[]{:S(2)}) %collective-permute-start.3) | collective-permute-done | bytes 819232 | tf_op jit(solution)/shard_map/ppermute | solution.py:676
  48.7 10.7 %other_part.7 = bf16[272,1280]{1,0:T(8,128)(2,1)} custom-call(s32[4]{0:T(128)} %refs_0_.9, s32[4,32]{1,0:T(4,128)} %refs_1_.9, s32[4,32]{1,0:T(4,128)} %refs_2_.9, bf16[320,1280]{1,0:T(8,128)(2,1)} %collective-permute-done.3.refs_3_.refs_4_, bf16[32,256,256]{2,1,0:T(8,128)(2,1)} %refs_7_.1, bf16[32,256,256]{2,1,0:T(8,128)(2,1)} %refs_8_.1), custom_call_target="tpu_custom_call" | custom-call | flops 5368709120 | bytes 1280 | tf_op jit(solution)/shard_map/other_part/pallas_call | solution.py:606
  59.4 5.6 %collective-permute-start.6 = (bf16[272,1280]{1,0:T(8,128)(2,1)}, bf16[272,1280]{1,0:T(8,128)(2,1)}, u32[]{:S(2)}, u32[]{:S(2)}) collective-permute-start(bf16[272,1280]{1,0:T(8,128)(2,1)} %other_part.7), channel_id=1, source_target_pairs={{0,8},{12,4},{1,9},{13,5},{2,10},{14,6},{3,11},{15,7},{16,24},{28,... | collective-permute-start | bytes 2088968 | tf_op jit(solution)/shard_map/ppermute | solution.py:676
  65.1 0.9 other_part.8
  66.0 1.3 %collective-permute-start.10 = (bf16[64,1280]{1,0:T(8,128)(2,1)}, bf16[64,1280]{1,0:T(8,128)(2,1)S(1)}, u32[]{:S(2)}, u32[]{:S(2)}) collective-permute-start(bf16[64,1280]{1,0:T(8,128)(2,1)} %get-tuple-element.50), channel_id=1, source_target_pairs={{4,0},{8,12},{5,1},{9,13},{6,2},{10,14},{7,3},{11,15},{20,16},{24,... | collective-permute-start | bytes 491528 | tf_op jit(solution)/shard_map/ppermute | solution.py:676
  67.3 2.6 %collective-permute-done.4.refs_4_ = bf16[16,256,256]{2,1,0:T(8,128)(2,1)} collective-permute-done((bf16[16,256,256]{2,1,0:T(8,128)(2,1)}, bf16[16,256,256]{2,1,0:T(8,128)(2,1)}, u32[]{:S(2)}, u32[]{:S(2)}) %collective-permute-start.4) | collective-permute-done | bytes 2097184 | tf_op jit(solution)/shard_map/ppermute | solution.py:676
  69.9 8.1 %collective-permute-start.9 = (bf16[272,1280]{1,0:T(8,128)(2,1)}, bf16[272,1280]{1,0:T(8,128)(2,1)}, u32[]{:S(2)}, u32[]{:S(2)}) collective-permute-start(bf16[272,1280]{1,0:T(8,128)(2,1)} %other_part.5), channel_id=1, source_target_pairs={{0,4},{12,8},{1,5},{13,9},{2,6},{14,10},{3,7},{15,11},{16,20},{28,... | collective-permute-start | bytes 2088968 | tf_op jit(solution)/shard_map/ppermute | solution.py:676
  78.0 0.9 other_part.9
  78.9 0.0 collective-permute-done.10.refs_5_
  78.9 0.0 copy-start
  79.0 1.3 %collective-permute-start.8 = (bf16[272,1280]{1,0:T(8,128)(2,1)}, bf16[272,1280]{1,0:T(8,128)(2,1)}, u32[]{:S(2)}, u32[]{:S(2)}) collective-permute-start(bf16[272,1280]{1,0:T(8,128)(2,1)} %other_part.9), channel_id=1, source_target_pairs={{4,12},{8,0},{5,13},{9,1},{6,14},{10,2},{7,15},{11,3},{20,28},{24,... | collective-permute-start | bytes 2088968 | tf_op jit(solution)/shard_map/ppermute | solution.py:676
  80.3 2.5 %push.1 = (bf16[2,160,256]{2,1,0:T(8,128)(2,1)}, bf16[2,160,256]{2,1,0:T(8,128)(2,1)}) custom-call(s32[4]{0:T(128)} %owner_ref.1, bf16[320,1280]{1,0:T(8,128)(2,1)} %prepare.1.payload_ref.refs_0_, bf16[320,1280]{1,0:T(8,128)(2,1)} %collective-permute-done.refs_4_.refs_3_.refs_1_, bf16[320,1280]{1,0:T(8,128)(2,1)} %collective-permute-done.1.refs_3_.refs_2_, ...), custom_call_target="tpu_custom_call" | custom-call | tf_op jit(solution)/shard_map/push/pallas_call | solution.py:732
  82.8 0.0 collective-permute-done.5.refs_0_
  82.8 2.1 %collective-permute-done.6.refs_1_ = bf16[272,1280]{1,0:T(8,128)(2,1)} collective-permute-done((bf16[272,1280]{1,0:T(8,128)(2,1)}, bf16[272,1280]{1,0:T(8,128)(2,1)}, u32[]{:S(2)}, u32[]{:S(2)}) %collective-permute-start.6) | collective-permute-done | bytes 696352 | tf_op jit(solution)/shard_map/ppermute | solution.py:676
  84.9 3.6 %combine.1 = (f32[256,1280]{1,0:T(8,128)}, f32[8,1280]{1,0:T(8,128)}) custom-call(f32[256,1280]{1,0:T(8,128)} %get-tuple-element.45.own_ref, f32[8,1280]{1,0:T(8,128)} %get-tuple-element.46.log_ref, bf16[272,1280]{1,0:T(8,128)(2,1)} %collective-permute-done.5.refs_0_, bf16[272,1280]{1,0:T(8,128)(2,1)} %collective-permute-done.6.refs_1_, ...), custom_call_target="tpu_custom_call" | custom-call | bytes 1280 | tf_op jit(solution)/shard_map/combine/pallas_call | solution.py:636
  88.5 10.2 %collective-permute-done.9.inner_ref = bf16[272,1280]{1,0:T(8,128)(2,1)} collective-permute-done((bf16[272,1280]{1,0:T(8,128)(2,1)}, bf16[272,1280]{1,0:T(8,128)(2,1)}, u32[]{:S(2)}, u32[]{:S(2)}) %collective-permute-start.9) | collective-permute-done | bytes 696352 | tf_op jit(solution)/shard_map/ppermute | solution.py:676
  98.7 5.5 %collective-permute-done.8.outer_ref = bf16[272,1280]{1,0:T(8,128)(2,1)} collective-permute-done((bf16[272,1280]{1,0:T(8,128)(2,1)}, bf16[272,1280]{1,0:T(8,128)(2,1)}, u32[]{:S(2)}, u32[]{:S(2)}) %collective-permute-start.8) | collective-permute-done | bytes 696352 | tf_op jit(solution)/shard_map/ppermute | solution.py:676
  104.1 3.3 %final.1 = bf16[160,2048]{1,0:T(8,128)(2,1)} custom-call(f32[256,1280]{1,0:T(8,128)} %get-tuple-element.47.own_ref, f32[8,1280]{1,0:T(8,128)} %get-tuple-element.48.log_ref, bf16[272,1280]{1,0:T(8,128)(2,1)} %collective-permute-done.8.outer_ref, bf16[272,1280]{1,0:T(8,128)(2,1)} %collective-permute-done.9.inner_ref), custom_call_target="tpu_custom_call" | custom-call | tf_op jit(solution)/shard_map/final/pallas_call | solution.py:648
  (3 shorter events, 0.0 us)
Async XLA Ops:
  3.0 24.3 %collective-permute-start = (bf16[320,1280]{1,0:T(8,128)(2,1)}, bf16[320,1280]{1,0:T(8,128)(2,1)}, u32[]{:S(2)}, u32[]{:S(2)}) collective-permute-start(bf16[320,1280]{1,0:T(8,128)(2,1)} %prepare.1.payload_ref.refs_0_), channel_id=1, source_target_pairs={{0,4},{4,0},{8,12},{12,8},{1,5},{5,1},{9,13},{13,9},{2,6},{6,2},{1... | collective-permute-start | bytes 2457608 | tf_op jit(solution)/shard_map/ppermute | solution.py:676
  6.0 21.3 %collective-permute-start.1 = (bf16[320,1280]{1,0:T(8,128)(2,1)}, bf16[320,1280]{1,0:T(8,128)(2,1)}, u32[]{:S(2)}, u32[]{:S(2)}) collective-permute-start(bf16[320,1280]{1,0:T(8,128)(2,1)} %prepare.1.payload_ref.refs_0_), channel_id=1, source_target_pairs={{4,8},{8,4},{5,9},{9,5},{6,10},{10,6},{7,11},{11,7},{20,24},{24,20... | collective-permute-start | bytes 2457608 | tf_op jit(solution)/shard_map/ppermute | solution.py:676
  11.5 58.4 %collective-permute-start.4 = (bf16[16,256,256]{2,1,0:T(8,128)(2,1)}, bf16[16,256,256]{2,1,0:T(8,128)(2,1)}, u32[]{:S(2)}, u32[]{:S(2)}) collective-permute-start(bf16[16,256,256]{2,1,0:T(8,128)(2,1)} %gather_blocks.1), channel_id=1, source_target_pairs={{0,4},{12,8},{1,5},{13,9},{2,6},{14,10},{3,7},{15,11},{16,20},{28,... | collective-permute-start | bytes 6291464 | tf_op jit(solution)/shard_map/ppermute | solution.py:676
  27.3 21.3 %collective-permute-start.3 = (bf16[320,1280]{1,0:T(8,128)(2,1)}, bf16[320,1280]{1,0:T(8,128)(2,1)}, u32[]{:S(2)}, u32[]{:S(2)}) collective-permute-start(bf16[320,1280]{1,0:T(8,128)(2,1)} %collective-permute-done.1.refs_3_.refs_2_), channel_id=1, source_target_pairs={{4,0},{8,12},{5,1},{9,13},{6,2},{10,14},{7,3},{11,15},{20,16},{24,... | collective-permute-start | bytes 2457608 | tf_op jit(solution)/shard_map/ppermute | solution.py:676
  28.6 36.4 %collective-permute-start.2 = (bf16[320,1280]{1,0:T(8,128)(2,1)}, bf16[320,1280]{1,0:T(8,128)(2,1)}, u32[]{:S(2)}, u32[]{:S(2)}) collective-permute-start(bf16[320,1280]{1,0:T(8,128)(2,1)} %collective-permute-done.refs_4_.refs_3_.refs_1_), channel_id=1, source_target_pairs={{4,8},{8,4},{5,9},{9,5},{6,10},{10,6},{7,11},{11,7},{20,24},{24,20... | collective-permute-start | bytes 2457608 | tf_op jit(solution)/shard_map/ppermute | solution.py:676
  41.7 41.1 %collective-permute-start.5 = (bf16[272,1280]{1,0:T(8,128)(2,1)}, bf16[272,1280]{1,0:T(8,128)(2,1)}, u32[]{:S(2)}, u32[]{:S(2)}) collective-permute-start(bf16[272,1280]{1,0:T(8,128)(2,1)} %other_part.5), channel_id=1, source_target_pairs={{4,8},{8,4},{5,9},{9,5},{6,10},{10,6},{7,11},{11,7},{20,24},{24,20... | collective-permute-start | bytes 2088968 | tf_op jit(solution)/shard_map/ppermute | solution.py:676
  43.3 39.5 %collective-permute-start.7 = (bf16[272,1280]{1,0:T(8,128)(2,1)}, bf16[272,1280]{1,0:T(8,128)(2,1)}, u32[]{:S(2)}, u32[]{:S(2)}) collective-permute-start(bf16[272,1280]{1,0:T(8,128)(2,1)} %other_part.6), channel_id=1, source_target_pairs={{4,0},{8,12},{5,1},{9,13},{6,2},{10,14},{7,3},{11,15},{20,16},{24,... | collective-permute-start | bytes 2088968 | tf_op jit(solution)/shard_map/ppermute | solution.py:676
  59.4 25.5 %collective-permute-start.6 = (bf16[272,1280]{1,0:T(8,128)(2,1)}, bf16[272,1280]{1,0:T(8,128)(2,1)}, u32[]{:S(2)}, u32[]{:S(2)}) collective-permute-start(bf16[272,1280]{1,0:T(8,128)(2,1)} %other_part.7), channel_id=1, source_target_pairs={{0,8},{12,4},{1,9},{13,5},{2,10},{14,6},{3,11},{15,7},{16,24},{28,... | collective-permute-start | bytes 2088968 | tf_op jit(solution)/shard_map/ppermute | solution.py:676
  66.0 12.9 %collective-permute-start.10 = (bf16[64,1280]{1,0:T(8,128)(2,1)}, bf16[64,1280]{1,0:T(8,128)(2,1)S(1)}, u32[]{:S(2)}, u32[]{:S(2)}) collective-permute-start(bf16[64,1280]{1,0:T(8,128)(2,1)} %get-tuple-element.50), channel_id=1, source_target_pairs={{4,0},{8,12},{5,1},{9,13},{6,2},{10,14},{7,3},{11,15},{20,16},{24,... | collective-permute-start | bytes 491528 | tf_op jit(solution)/shard_map/ppermute | solution.py:676
  69.9 28.7 %collective-permute-start.9 = (bf16[272,1280]{1,0:T(8,128)(2,1)}, bf16[272,1280]{1,0:T(8,128)(2,1)}, u32[]{:S(2)}, u32[]{:S(2)}) collective-permute-start(bf16[272,1280]{1,0:T(8,128)(2,1)} %other_part.5), channel_id=1, source_target_pairs={{0,4},{12,8},{1,5},{13,9},{2,6},{14,10},{3,7},{15,11},{16,20},{28,... | collective-permute-start | bytes 2088968 | tf_op jit(solution)/shard_map/ppermute | solution.py:676
  78.9 1.3 %copy-start = (bf16[64,1280]{1,0:T(8,128)(2,1)}, bf16[64,1280]{1,0:T(8,128)(2,1)S(1)}, u32[]{:S(2)}) copy-start(bf16[64,1280]{1,0:T(8,128)(2,1)S(1)} %collective-permute-done.10.refs_5_) | copy-start | bytes 491524
  79.0 25.2 %collective-permute-start.8 = (bf16[272,1280]{1,0:T(8,128)(2,1)}, bf16[272,1280]{1,0:T(8,128)(2,1)}, u32[]{:S(2)}, u32[]{:S(2)}) collective-permute-start(bf16[272,1280]{1,0:T(8,128)(2,1)} %other_part.9), channel_id=1, source_target_pairs={{4,12},{8,0},{5,13},{9,1},{6,14},{10,2},{7,15},{11,3},{20,28},{24,... | collective-permute-start | bytes 2088968 | tf_op jit(solution)/shard_map/ppermute | solution.py:676

commit v2 on v1

--- a/solution.py
+++ b/solution.py
@@ -197,22 +197,58 @@
     return outs, logs
 
 
-def prepare_kernel(query_ref, new_key_ref, new_value_ref, payload_ref, query_rows):
+def prepare_kernel(
+    query_ref, new_key_ref, new_value_ref, payload_ref, query_buf, query_rows, payload_buf, sems
+):
     new_rows = query_ref.shape[0]
     kv_width = new_key_ref.shape[1]
-    for kv in range(kv_width // HD):
+    kv_local = kv_width // HD
+    lanes = GROUP * HD
+    pieces = new_rows // PIECE
+    coming = [
+        pltpu.make_async_copy(
+            query_ref.at[:, kv * lanes : (kv + 1) * lanes],
+            query_buf.at[:, kv * lanes : (kv + 1) * lanes],
+            sems.at[0, kv],
+        )
+        for kv in range(kv_local)
+    ]
+    for i, new_ref in enumerate((new_key_ref, new_value_ref)):
+        for piece in range(pieces):
+            row, lane = piece_place(i, piece, new_rows, kv_width)
+            coming.append(
+                pltpu.make_async_copy(
+                    new_ref.at[piece * PIECE : (piece + 1) * PIECE],
+                    payload_buf.at[row : row + PIECE, lane : lane + kv_width],
+                    sems.at[0, kv_local + i * pieces + piece],
+                )
+            )
+    for copy in coming:
+        copy.start()
+    leaving = []
+
+    def leave(start, stop):
+        leaving.append(
+            pltpu.make_async_copy(
+                payload_buf.at[start:stop], payload_ref.at[start:stop], sems.at[1, len(leaving)]
+            )
+        )
+        leaving[-1].start()
+
+    for kv in range(kv_local):
+        coming[kv].wait()
         for g in range(GROUP):
             head = kv * GROUP + g
-            query_rows[g * new_rows : (g + 1) * new_rows, :] = query_ref[
+            query_rows[kv, g * new_rows : (g + 1) * new_rows, :] = query_buf[
                 :, head * HD : (head + 1) * HD
             ]
-        payload_ref[kv * HD : (kv + 1) * HD, :] = query_rows[...].T
-    for i, new_ref in enumerate((new_key_ref, new_value_ref)):
-        for piece in range(new_rows // PIECE):
-            row, lane = piece_place(i, piece, new_rows, kv_width)
-            payload_ref[row : row + PIECE, lane : lane + kv_width] = new_ref[
-                piece * PIECE : (piece + 1) * PIECE, :
-            ]
+        payload_buf[kv * HD : (kv + 1) * HD, :] = query_rows[kv].T
+        leave(kv * HD, (kv + 1) * HD)
+    for copy in coming[kv_local:]:
+        copy.wait()
+    leave(kv_width, payload_buf.shape[0])
+    for copy in leaving:
+        copy.wait()
 
 
 def piece_place(i, piece, new_rows, kv_width):
@@ -663,9 +699,14 @@
 
     payload = pl.pallas_call(
         prepare_kernel,
-        in_specs=[vmem_spec] * 3,
-        out_specs=vmem_spec,
-        scratch_shapes=[pltpu.VMEM((rows, HD), jnp.bfloat16)],
+        in_specs=[hbm_spec] * 3,
+        out_specs=hbm_spec,
+        scratch_shapes=[
+            pltpu.VMEM((new_rows, width), jnp.bfloat16),
+            pltpu.VMEM((kv_local, rows, HD), jnp.bfloat16),
+            pltpu.VMEM((payload_rows(new_rows, kv_width), rows), jnp.bfloat16),
+            pltpu.SemaphoreType.DMA((2, kv_local + 2 * (new_rows // PIECE))),
+        ],
         out_shape=jax.ShapeDtypeStruct((payload_rows(new_rows, kv_width), rows), jnp.bfloat16),
         compiler_params=params,
         name="prepare",

time: 107 us -> 106 us (level); the launches traced: 108 us -> 105 us
  Pallas kernels: 50.5 us -> 44.8 us
  waiting for transfers between devices: 24.5 us -> 29 us
  starting transfers between devices: 31.7 us -> 30.5 us
    ppermute x11, waiting for transfers between devices: 24.5 us -> 29 us  [send(): return lax.ppermute(array, 'pool', pairs)]
    pallas_call x1, Pallas kernels: 10.8 us -> 7.72 us  [own_part(): pl.pallas_call(functools.partial(own_kernel, pool_size), in_specs=[smem_s...]
    pallas_call x5, Pallas kernels: 24.1 us -> 21.5 us  [other_part(): pl.pallas_call(functools.partial(other_kernel, pool_size, new_rows, partn...]
    ppermute x11, starting transfers between devices: 31.7 us -> 30.5 us  [send(): return lax.ppermute(array, 'pool', pairs)]
  transfers between devices with their start and end apart: 11 -> 11, of which waited for: 5 -> 6; matrix products, arithmetic and copies ran while one was open for 0% -> 0% of each run, Pallas kernels for 42% -> 37%
where the time goes in v2:
time: 106 us; the launch traced here: 105 us
  Pallas kernels  44.8 us (42%)
  starting transfers between devices  30.5 us (29%)
  waiting for transfers between devices  29 us (27%)
    ppermute x11, starting transfers between devices, send(): return lax.ppermute(array, 'pool', pairs)  30.5 us
    ppermute x11, waiting for transfers between devices, send(): return lax.ppermute(array, 'pool', pairs)  29 us
    pallas_call x5, Pallas kernels, other_part(): pl.pallas_call(functools.partial(other_kernel, pool_size, new_rows, partn...  21.5 us
    pallas_call x1, Pallas kernels, own_part(): pl.pallas_call(functools.partial(own_kernel, pool_size), in_specs=[smem_s...  7.72 us
    pallas_call x1, Pallas kernels, shards(): pl.pallas_call(functools.partial(gather_kernel, pool_size), in_specs=[sme...  3.83 us
    pallas_call x1, Pallas kernels, combine(): pl.pallas_call(functools.partial(combine_kernel, tuple(sources), last), i...  3.61 us
    pallas_call x1, Pallas kernels, final(): pl.pallas_call(final_kernel, in_specs=[hbm_spec, vmem_spec, hbm_spec, hbm...  3.33 us
    pallas_call x1, Pallas kernels, shards(): pl.pallas_call(functools.partial(push_kernel, pool_size, tuple((entry for...  2.61 us
  transfers between devices with their start and end apart: 11, of which 6 were waited for; matrix products, arithmetic and copies ran while one was open for 0% of the time, Pallas kernels for 37%

profile of v2, /device:TPU:0, one launch (start us, length us, event | category | flops | bytes accessed | tf_op | source)
XLA Modules:
  0.0 105.3 jit_solution(9672999254194290361)
XLA Ops:
  0.6 2.3 %prepare.1.payload_ref.refs_0_ = bf16[320,1280]{1,0:T(8,128)(2,1)} custom-call(bf16[160,2048]{1,0:T(8,128)(2,1)} %bitcast.4, bf16[160,256]{1,0:T(8,128)(2,1)} %bitcast.6, bf16[160,256]{1,0:T(8,128)(2,1)} %bitcast.8), custom_call_target="tpu_custom_call" | custom-call | tf_op jit(solution)/shard_map/prepare/pallas_call | solution.py:700
  2.9 3.1 %collective-permute-start = (bf16[320,1280]{1,0:T(8,128)(2,1)}, bf16[320,1280]{1,0:T(8,128)(2,1)}, u32[]{:S(2)}, u32[]{:S(2)}) collective-permute-start(bf16[320,1280]{1,0:T(8,128)(2,1)} %prepare.1.payload_ref.refs_0_), channel_id=1, source_target_pairs={{0,4},{4,0},{8,12},{12,8},{1,5},{5,1},{9,13},{13,9},{2,6},{6,2},{1... | collective-permute-start | bytes 2457608 | tf_op jit(solution)/shard_map/ppermute | solution.py:717
  6.0 1.7 %collective-permute-start.1 = (bf16[320,1280]{1,0:T(8,128)(2,1)}, bf16[320,1280]{1,0:T(8,128)(2,1)}, u32[]{:S(2)}, u32[]{:S(2)}) collective-permute-start(bf16[320,1280]{1,0:T(8,128)(2,1)} %prepare.1.payload_ref.refs_0_), channel_id=1, source_target_pairs={{4,8},{8,4},{5,9},{9,5},{6,10},{10,6},{7,11},{11,7},{20,24},{24,20... | collective-permute-start | bytes 2457608 | tf_op jit(solution)/shard_map/ppermute | solution.py:717
  7.7 3.8 %gather_blocks.1 = bf16[16,256,256]{2,1,0:T(8,128)(2,1)} custom-call(s32[4]{0:T(128)} %refs_0_.9, s32[4,32]{1,0:T(4,128)} %refs_1_.9, s32[4,32]{1,0:T(4,128)} %refs_2_.9, bf16[32,256,256]{2,1,0:T(8,128)(2,1)} %refs_7_.1, bf16[32,256,256]{2,1,0:T(8,128)(2,1)} %refs_8_.1), custom_call_target="tpu_custom_call" | custom-call | tf_op jit(solution)/shard_map/gather_blocks/pallas_call | solution.py:721
  11.5 5.0 %collective-permute-start.4 = (bf16[16,256,256]{2,1,0:T(8,128)(2,1)}, bf16[16,256,256]{2,1,0:T(8,128)(2,1)}, u32[]{:S(2)}, u32[]{:S(2)}) collective-permute-start(bf16[16,256,256]{2,1,0:T(8,128)(2,1)} %gather_blocks.1), channel_id=1, source_target_pairs={{0,4},{12,8},{1,5},{13,9},{2,6},{14,10},{3,7},{15,11},{16,20},{28,... | collective-permute-start | bytes 6291464 | tf_op jit(solution)/shard_map/ppermute | solution.py:717
  16.5 7.7 %own_part.1 = (f32[256,1280]{1,0:T(8,128)}, f32[8,1280]{1,0:T(8,128)}) custom-call(s32[4]{0:T(128)} %refs_0_.9, s32[4,32]{1,0:T(4,128)} %refs_1_.9, s32[4,32]{1,0:T(4,128)} %refs_2_.9, bf16[320,1280]{1,0:T(8,128)(2,1)} %prepare.1.payload_ref.refs_0_, bf16[160,256]{1,0:T(8,128)(2,1)} %bitcast.7, bf16[160,256]{1,0:T(8,128)(2,1)} %bitcast.9, ...), custom_call_target="tpu_custom_call" | custom-call | flops 5368709120 | bytes 1280 | tf_op jit(solution)/shard_map/own_part/pallas_call | solution.py:613
  24.3 0.7 collective-permute-done.refs_4_.refs_3_.refs_1_
  25.0 0.0 collective-permute-done.1.refs_3_.refs_2_
  25.0 1.3 %collective-permute-start.3 = (bf16[320,1280]{1,0:T(8,128)(2,1)}, bf16[320,1280]{1,0:T(8,128)(2,1)}, u32[]{:S(2)}, u32[]{:S(2)}) collective-permute-start(bf16[320,1280]{1,0:T(8,128)(2,1)} %collective-permute-done.1.refs_3_.refs_2_), channel_id=1, source_target_pairs={{4,0},{8,12},{5,1},{9,13},{6,2},{10,14},{7,3},{11,15},{20,16},{24,... | collective-permute-start | bytes 2457608 | tf_op jit(solution)/shard_map/ppermute | solution.py:717
  26.3 1.6 %collective-permute-start.2 = (bf16[320,1280]{1,0:T(8,128)(2,1)}, bf16[320,1280]{1,0:T(8,128)(2,1)}, u32[]{:S(2)}, u32[]{:S(2)}) collective-permute-start(bf16[320,1280]{1,0:T(8,128)(2,1)} %collective-permute-done.refs_4_.refs_3_.refs_1_), channel_id=1, source_target_pairs={{4,8},{8,4},{5,9},{9,5},{6,10},{10,6},{7,11},{11,7},{20,24},{24,20... | collective-permute-start | bytes 2457608 | tf_op jit(solution)/shard_map/ppermute | solution.py:717
  27.8 8.7 %other_part.5 = bf16[272,1280]{1,0:T(8,128)(2,1)} custom-call(s32[4]{0:T(128)} %refs_0_.9, s32[4,32]{1,0:T(4,128)} %refs_1_.9, s32[4,32]{1,0:T(4,128)} %refs_2_.9, bf16[320,1280]{1,0:T(8,128)(2,1)} %collective-permute-done.1.refs_3_.refs_2_, bf16[320,1280]{1,0:T(8,128)(2,1)} %collective-permute-done.refs_4_.refs_3_.refs_1_, bf16[32,256,256]{2,1,0:T(8,128)(2,1)} %refs_7_.1, ...), custom_call_target="tpu_custom_call" | custom-call | flops 5368709120 | bytes 1280 | tf_op jit(solution)/shard_map/other_part/pallas_call | solution.py:642
  36.5 0.9 other_part.6
  37.5 1.6 %collective-permute-start.5 = (bf16[272,1280]{1,0:T(8,128)(2,1)}, bf16[272,1280]{1,0:T(8,128)(2,1)}, u32[]{:S(2)}, u32[]{:S(2)}) collective-permute-start(bf16[272,1280]{1,0:T(8,128)(2,1)} %other_part.5), channel_id=1, source_target_pairs={{4,8},{8,4},{5,9},{9,5},{6,10},{10,6},{7,11},{11,7},{20,24},{24,20... | collective-permute-start | bytes 2088968 | tf_op jit(solution)/shard_map/ppermute | solution.py:717
  39.0 1.3 %collective-permute-start.7 = (bf16[272,1280]{1,0:T(8,128)(2,1)}, bf16[272,1280]{1,0:T(8,128)(2,1)}, u32[]{:S(2)}, u32[]{:S(2)}) collective-permute-start(bf16[272,1280]{1,0:T(8,128)(2,1)} %other_part.6), channel_id=1, source_target_pairs={{4,0},{8,12},{5,1},{9,13},{6,2},{10,14},{7,3},{11,15},{20,16},{24,... | collective-permute-start | bytes 2088968 | tf_op jit(solution)/shard_map/ppermute | solution.py:717
  40.3 8.0 %collective-permute-done.3.refs_3_.refs_4_ = bf16[320,1280]{1,0:T(8,128)(2,1)} collective-permute-done((bf16[320,1280]{1,0:T(8,128)(2,1)}, bf16[320,1280]{1,0:T(8,128)(2,1)}, u32[]{:S(2)}, u32[]{:S(2)}) %collective-permute-start.3) | collective-permute-done | bytes 819232 | tf_op jit(solution)/shard_map/ppermute | solution.py:717
  48.3 10.0 %other_part.7 = bf16[272,1280]{1,0:T(8,128)(2,1)} custom-call(s32[4]{0:T(128)} %refs_0_.9, s32[4,32]{1,0:T(4,128)} %refs_1_.9, s32[4,32]{1,0:T(4,128)} %refs_2_.9, bf16[320,1280]{1,0:T(8,128)(2,1)} %collective-permute-done.3.refs_3_.refs_4_, bf16[32,256,256]{2,1,0:T(8,128)(2,1)} %refs_7_.1, bf16[32,256,256]{2,1,0:T(8,128)(2,1)} %refs_8_.1), custom_call_target="tpu_custom_call" | custom-call | flops 5368709120 | bytes 1280 | tf_op jit(solution)/shard_map/other_part/pallas_call | solution.py:642
  58.3 5.1 %collective-permute-start.6 = (bf16[272,1280]{1,0:T(8,128)(2,1)}, bf16[272,1280]{1,0:T(8,128)(2,1)}, u32[]{:S(2)}, u32[]{:S(2)}) collective-permute-start(bf16[272,1280]{1,0:T(8,128)(2,1)} %other_part.7), channel_id=1, source_target_pairs={{0,8},{12,4},{1,9},{13,5},{2,10},{14,6},{3,11},{15,7},{16,24},{28,... | collective-permute-start | bytes 2088968 | tf_op jit(solution)/shard_map/ppermute | solution.py:717
  63.3 0.0 collective-permute-done.2.refs_3_
  63.3 0.9 other_part.8
  64.3 1.3 %collective-permute-start.10 = (bf16[64,1280]{1,0:T(8,128)(2,1)}, bf16[64,1280]{1,0:T(8,128)(2,1)S(1)}, u32[]{:S(2)}, u32[]{:S(2)}) collective-permute-start(bf16[64,1280]{1,0:T(8,128)(2,1)} %get-tuple-element.50), channel_id=1, source_target_pairs={{4,0},{8,12},{5,1},{9,13},{6,2},{10,14},{7,3},{11,15},{20,16},{24,... | collective-permute-start | bytes 491528 | tf_op jit(solution)/shard_map/ppermute | solution.py:717
  65.6 4.3 %collective-permute-done.4.refs_4_ = bf16[16,256,256]{2,1,0:T(8,128)(2,1)} collective-permute-done((bf16[16,256,256]{2,1,0:T(8,128)(2,1)}, bf16[16,256,256]{2,1,0:T(8,128)(2,1)}, u32[]{:S(2)}, u32[]{:S(2)}) %collective-permute-start.4) | collective-permute-done | bytes 2097184 | tf_op jit(solution)/shard_map/ppermute | solution.py:717
  69.9 7.4 %collective-permute-start.9 = (bf16[272,1280]{1,0:T(8,128)(2,1)}, bf16[272,1280]{1,0:T(8,128)(2,1)}, u32[]{:S(2)}, u32[]{:S(2)}) collective-permute-start(bf16[272,1280]{1,0:T(8,128)(2,1)} %other_part.5), channel_id=1, source_target_pairs={{0,4},{12,8},{1,5},{13,9},{2,6},{14,10},{3,7},{15,11},{16,20},{28,... | collective-permute-start | bytes 2088968 | tf_op jit(solution)/shard_map/ppermute | solution.py:717
  77.3 0.9 other_part.9
  78.3 0.0 copy-start
  78.3 1.3 %collective-permute-start.8 = (bf16[272,1280]{1,0:T(8,128)(2,1)}, bf16[272,1280]{1,0:T(8,128)(2,1)}, u32[]{:S(2)}, u32[]{:S(2)}) collective-permute-start(bf16[272,1280]{1,0:T(8,128)(2,1)} %other_part.9), channel_id=1, source_target_pairs={{4,12},{8,0},{5,13},{9,1},{6,14},{10,2},{7,15},{11,3},{20,28},{24,... | collective-permute-start | bytes 2088968 | tf_op jit(solution)/shard_map/ppermute | solution.py:717
  79.6 2.6 %push.1 = (bf16[2,160,256]{2,1,0:T(8,128)(2,1)}, bf16[2,160,256]{2,1,0:T(8,128)(2,1)}) custom-call(s32[4]{0:T(128)} %owner_ref.1, bf16[320,1280]{1,0:T(8,128)(2,1)} %prepare.1.payload_ref.refs_0_, bf16[320,1280]{1,0:T(8,128)(2,1)} %collective-permute-done.refs_4_.refs_3_.refs_1_, bf16[320,1280]{1,0:T(8,128)(2,1)} %collective-permute-done.1.refs_3_.refs_2_, ...), custom_call_target="tpu_custom_call" | custom-call | tf_op jit(solution)/shard_map/push/pallas_call | solution.py:773
  82.2 0.0 collective-permute-done.7.refs_2_
  82.2 2.6 %collective-permute-done.6.refs_1_ = bf16[272,1280]{1,0:T(8,128)(2,1)} collective-permute-done((bf16[272,1280]{1,0:T(8,128)(2,1)}, bf16[272,1280]{1,0:T(8,128)(2,1)}, u32[]{:S(2)}, u32[]{:S(2)}) %collective-permute-start.6) | collective-permute-done | bytes 696352 | tf_op jit(solution)/shard_map/ppermute | solution.py:717
  84.9 3.6 %combine.1 = (f32[256,1280]{1,0:T(8,128)}, f32[8,1280]{1,0:T(8,128)}) custom-call(f32[256,1280]{1,0:T(8,128)} %get-tuple-element.45.own_ref, f32[8,1280]{1,0:T(8,128)} %get-tuple-element.46.log_ref, bf16[272,1280]{1,0:T(8,128)(2,1)} %collective-permute-done.5.refs_0_, bf16[272,1280]{1,0:T(8,128)(2,1)} %collective-permute-done.6.refs_1_, ...), custom_call_target="tpu_custom_call" | custom-call | bytes 1280 | tf_op jit(solution)/shard_map/combine/pallas_call | solution.py:672
  88.5 10.2 %collective-permute-done.9.inner_ref = bf16[272,1280]{1,0:T(8,128)(2,1)} collective-permute-done((bf16[272,1280]{1,0:T(8,128)(2,1)}, bf16[272,1280]{1,0:T(8,128)(2,1)}, u32[]{:S(2)}, u32[]{:S(2)}) %collective-permute-start.9) | collective-permute-done | bytes 696352 | tf_op jit(solution)/shard_map/ppermute | solution.py:717
  98.7 3.2 %collective-permute-done.8.outer_ref = bf16[272,1280]{1,0:T(8,128)(2,1)} collective-permute-done((bf16[272,1280]{1,0:T(8,128)(2,1)}, bf16[272,1280]{1,0:T(8,128)(2,1)}, u32[]{:S(2)}, u32[]{:S(2)}) %collective-permute-start.8) | collective-permute-done | bytes 696352 | tf_op jit(solution)/shard_map/ppermute | solution.py:717
  101.8 3.3 %final.1 = bf16[160,2048]{1,0:T(8,128)(2,1)} custom-call(f32[256,1280]{1,0:T(8,128)} %get-tuple-element.47.own_ref, f32[8,1280]{1,0:T(8,128)} %get-tuple-element.48.log_ref, bf16[272,1280]{1,0:T(8,128)(2,1)} %collective-permute-done.8.outer_ref, bf16[272,1280]{1,0:T(8,128)(2,1)} %collective-permute-done.9.inner_ref), custom_call_target="tpu_custom_call" | custom-call | tf_op jit(solution)/shard_map/final/pallas_call | solution.py:684
  (3 shorter events, 0.0 us)
Async XLA Ops:
  2.9 22.1 %collective-permute-start = (bf16[320,1280]{1,0:T(8,128)(2,1)}, bf16[320,1280]{1,0:T(8,128)(2,1)}, u32[]{:S(2)}, u32[]{:S(2)}) collective-permute-start(bf16[320,1280]{1,0:T(8,128)(2,1)} %prepare.1.payload_ref.refs_0_), channel_id=1, source_target_pairs={{0,4},{4,0},{8,12},{12,8},{1,5},{5,1},{9,13},{13,9},{2,6},{6,2},{1... | collective-permute-start | bytes 2457608 | tf_op jit(solution)/shard_map/ppermute | solution.py:717
  6.0 19.0 %collective-permute-start.1 = (bf16[320,1280]{1,0:T(8,128)(2,1)}, bf16[320,1280]{1,0:T(8,128)(2,1)}, u32[]{:S(2)}, u32[]{:S(2)}) collective-permute-start(bf16[320,1280]{1,0:T(8,128)(2,1)} %prepare.1.payload_ref.refs_0_), channel_id=1, source_target_pairs={{4,8},{8,4},{5,9},{9,5},{6,10},{10,6},{7,11},{11,7},{20,24},{24,20... | collective-permute-start | bytes 2457608 | tf_op jit(solution)/shard_map/ppermute | solution.py:717
  11.5 58.4 %collective-permute-start.4 = (bf16[16,256,256]{2,1,0:T(8,128)(2,1)}, bf16[16,256,256]{2,1,0:T(8,128)(2,1)}, u32[]{:S(2)}, u32[]{:S(2)}) collective-permute-start(bf16[16,256,256]{2,1,0:T(8,128)(2,1)} %gather_blocks.1), channel_id=1, source_target_pairs={{0,4},{12,8},{1,5},{13,9},{2,6},{14,10},{3,7},{15,11},{16,20},{28,... | collective-permute-start | bytes 6291464 | tf_op jit(solution)/shard_map/ppermute | solution.py:717
  25.0 23.3 %collective-permute-start.3 = (bf16[320,1280]{1,0:T(8,128)(2,1)}, bf16[320,1280]{1,0:T(8,128)(2,1)}, u32[]{:S(2)}, u32[]{:S(2)}) collective-permute-start(bf16[320,1280]{1,0:T(8,128)(2,1)} %collective-permute-done.1.refs_3_.refs_2_), channel_id=1, source_target_pairs={{4,0},{8,12},{5,1},{9,13},{6,2},{10,14},{7,3},{11,15},{20,16},{24,... | collective-permute-start | bytes 2457608 | tf_op jit(solution)/shard_map/ppermute | solution.py:717
  26.3 37.1 %collective-permute-start.2 = (bf16[320,1280]{1,0:T(8,128)(2,1)}, bf16[320,1280]{1,0:T(8,128)(2,1)}, u32[]{:S(2)}, u32[]{:S(2)}) collective-permute-start(bf16[320,1280]{1,0:T(8,128)(2,1)} %collective-permute-done.refs_4_.refs_3_.refs_1_), channel_id=1, source_target_pairs={{4,8},{8,4},{5,9},{9,5},{6,10},{10,6},{7,11},{11,7},{20,24},{24,20... | collective-permute-start | bytes 2457608 | tf_op jit(solution)/shard_map/ppermute | solution.py:717
  37.5 44.8 %collective-permute-start.5 = (bf16[272,1280]{1,0:T(8,128)(2,1)}, bf16[272,1280]{1,0:T(8,128)(2,1)}, u32[]{:S(2)}, u32[]{:S(2)}) collective-permute-start(bf16[272,1280]{1,0:T(8,128)(2,1)} %other_part.5), channel_id=1, source_target_pairs={{4,8},{8,4},{5,9},{9,5},{6,10},{10,6},{7,11},{11,7},{20,24},{24,20... | collective-permute-start | bytes 2088968 | tf_op jit(solution)/shard_map/ppermute | solution.py:717
  39.0 43.2 %collective-permute-start.7 = (bf16[272,1280]{1,0:T(8,128)(2,1)}, bf16[272,1280]{1,0:T(8,128)(2,1)}, u32[]{:S(2)}, u32[]{:S(2)}) collective-permute-start(bf16[272,1280]{1,0:T(8,128)(2,1)} %other_part.6), channel_id=1, source_target_pairs={{4,0},{8,12},{5,1},{9,13},{6,2},{10,14},{7,3},{11,15},{20,16},{24,... | collective-permute-start | bytes 2088968 | tf_op jit(solution)/shard_map/ppermute | solution.py:717
  58.3 26.6 %collective-permute-start.6 = (bf16[272,1280]{1,0:T(8,128)(2,1)}, bf16[272,1280]{1,0:T(8,128)(2,1)}, u32[]{:S(2)}, u32[]{:S(2)}) collective-permute-start(bf16[272,1280]{1,0:T(8,128)(2,1)} %other_part.7), channel_id=1, source_target_pairs={{0,8},{12,4},{1,9},{13,5},{2,10},{14,6},{3,11},{15,7},{16,24},{28,... | collective-permute-start | bytes 2088968 | tf_op jit(solution)/shard_map/ppermute | solution.py:717
  64.3 14.0 %collective-permute-start.10 = (bf16[64,1280]{1,0:T(8,128)(2,1)}, bf16[64,1280]{1,0:T(8,128)(2,1)S(1)}, u32[]{:S(2)}, u32[]{:S(2)}) collective-permute-start(bf16[64,1280]{1,0:T(8,128)(2,1)} %get-tuple-element.50), channel_id=1, source_target_pairs={{4,0},{8,12},{5,1},{9,13},{6,2},{10,14},{7,3},{11,15},{20,16},{24,... | collective-permute-start | bytes 491528 | tf_op jit(solution)/shard_map/ppermute | solution.py:717
  69.9 28.7 %collective-permute-start.9 = (bf16[272,1280]{1,0:T(8,128)(2,1)}, bf16[272,1280]{1,0:T(8,128)(2,1)}, u32[]{:S(2)}, u32[]{:S(2)}) collective-permute-start(bf16[272,1280]{1,0:T(8,128)(2,1)} %other_part.5), channel_id=1, source_target_pairs={{0,4},{12,8},{1,5},{13,9},{2,6},{14,10},{3,7},{15,11},{16,20},{28,... | collective-permute-start | bytes 2088968 | tf_op jit(solution)/shard_map/ppermute | solution.py:717
  78.3 1.3 %copy-start = (bf16[64,1280]{1,0:T(8,128)(2,1)}, bf16[64,1280]{1,0:T(8,128)(2,1)S(1)}, u32[]{:S(2)}) copy-start(bf16[64,1280]{1,0:T(8,128)(2,1)S(1)} %collective-permute-done.10.refs_5_) | copy-start | bytes 491524
  78.3 23.5 %collective-permute-start.8 = (bf16[272,1280]{1,0:T(8,128)(2,1)}, bf16[272,1280]{1,0:T(8,128)(2,1)}, u32[]{:S(2)}, u32[]{:S(2)}) collective-permute-start(bf16[272,1280]{1,0:T(8,128)(2,1)} %other_part.9), channel_id=1, source_target_pairs={{4,12},{8,0},{5,13},{9,1},{6,14},{10,2},{7,15},{11,3},{20,28},{24,... | collective-permute-start | bytes 2088968 | tf_op jit(solution)/shard_map/ppermute | solution.py:717

commit v3 on v1

--- a/solution.py
+++ b/solution.py
@@ -297,6 +297,22 @@
                 query_copy(payload_ref).start()
             else:
                 pl.when(hit)(query_copy(payload_ref).start)
+        if raw:
+            passed = pltpu.make_async_copy(
+                payload_refs[0].at[kv_width:], results_ref[2], out_sem.at[2]
+            )
+            passed.start()
+        restore = None
+        if initial is not None:
+
+            def restore(*targets):
+                return [
+                    pltpu.make_async_copy(source, target, out_sem.at[i])
+                    for i, (source, target) in enumerate(zip(initial, targets))
+                ]
+
+            for copy in restore(work[-1], work[2]):
+                copy.start()
         count, ready = fetch(
             pool_size,
             tables,
@@ -306,22 +322,6 @@
             sems,
             moved,
         )
-        if raw:
-            passed = pltpu.make_async_copy(
-                payload_refs[0].at[kv_width:], results_ref[2], out_sem.at[2]
-            )
-            passed.start()
-        restore = None
-        if initial is not None:
-
-            def restore(*targets):
-                return [
-                    pltpu.make_async_copy(source, target, out_sem.at[i])
-                    for i, (source, target) in enumerate(zip(initial, targets))
-                ]
-
-            for copy in restore(work[-1], work[2]):
-                copy.start()
         query_copy(payload_refs[0]).wait()
         results = attend(
             key_buf, value_buf, count, ready, None, new_rows, columns, *work, restore, raw

time: 107 us -> 106 us (level); the launches traced: 108 us -> 105 us
  Pallas kernels: 50.5 us -> 40.9 us
  waiting for transfers between devices: 24.5 us -> 32.8 us
  starting transfers between devices: 31.7 us -> 30.4 us
    ppermute x11, waiting for transfers between devices: 24.5 us -> 32.8 us  [send(): return lax.ppermute(array, 'pool', pairs)]
    pallas_call x1, Pallas kernels: 10.8 us -> 5.81 us  [own_part(): pl.pallas_call(functools.partial(own_kernel, pool_size), in_specs=[smem_s...]
    pallas_call x5, Pallas kernels: 24.1 us -> 19.6 us  [other_part(): pl.pallas_call(functools.partial(other_kernel, pool_size, new_rows, partn...]
    ppermute x11, starting transfers between devices: 31.7 us -> 30.4 us  [send(): return lax.ppermute(array, 'pool', pairs)]
  transfers between devices with their start and end apart: 11 -> 11, of which waited for: 5 -> 6; matrix products, arithmetic and copies ran while one was open for 0% -> 0% of each run, Pallas kernels for 42% -> 34%
where the time goes in v3:
time: 106 us; the launch traced here: 105 us
  Pallas kernels  40.9 us (39%)
  waiting for transfers between devices  32.8 us (31%)
  starting transfers between devices  30.4 us (29%)
    ppermute x11, waiting for transfers between devices, send(): return lax.ppermute(array, 'pool', pairs)  32.8 us
    ppermute x11, starting transfers between devices, send(): return lax.ppermute(array, 'pool', pairs)  30.4 us
    pallas_call x5, Pallas kernels, other_part(): pl.pallas_call(functools.partial(other_kernel, pool_size, new_rows, partn...  19.6 us
    pallas_call x1, Pallas kernels, own_part(): pl.pallas_call(functools.partial(own_kernel, pool_size), in_specs=[smem_s...  5.81 us
    pallas_call x1, Pallas kernels, combine(): pl.pallas_call(functools.partial(combine_kernel, tuple(sources), last), i...  3.61 us
    pallas_call x1, Pallas kernels, shards(): pl.pallas_call(functools.partial(gather_kernel, pool_size), in_specs=[sme...  3.59 us
    pallas_call x1, Pallas kernels, final(): pl.pallas_call(final_kernel, in_specs=[hbm_spec, vmem_spec, hbm_spec, hbm...  3.33 us
    pallas_call x1, Pallas kernels, shards(): pl.pallas_call(functools.partial(push_kernel, pool_size, tuple((entry for...  2.63 us
  transfers between devices with their start and end apart: 11, of which 6 were waited for; matrix products, arithmetic and copies ran while one was open for 0% of the time, Pallas kernels for 34%

profile of v3, /device:TPU:0, one launch (start us, length us, event | category | flops | bytes accessed | tf_op | source)
XLA Modules:
  0.0 105.0 jit_solution(12190374333218076454)
XLA Ops:
  0.6 2.4 %prepare.1.payload_ref.refs_0_ = bf16[320,1280]{1,0:T(8,128)(2,1)} custom-call(bf16[160,2048]{1,0:T(8,128)(2,1)} %bitcast.4, bf16[160,256]{1,0:T(8,128)(2,1)} %bitcast.6, bf16[160,256]{1,0:T(8,128)(2,1)} %bitcast.8), custom_call_target="tpu_custom_call" | custom-call | tf_op jit(solution)/shard_map/prepare/pallas_call | solution.py:664
  3.0 3.0 %collective-permute-start = (bf16[320,1280]{1,0:T(8,128)(2,1)}, bf16[320,1280]{1,0:T(8,128)(2,1)}, u32[]{:S(2)}, u32[]{:S(2)}) collective-permute-start(bf16[320,1280]{1,0:T(8,128)(2,1)} %prepare.1.payload_ref.refs_0_), channel_id=1, source_target_pairs={{0,4},{4,0},{8,12},{12,8},{1,5},{5,1},{9,13},{13,9},{2,6},{6,2},{1... | collective-permute-start | bytes 2457608 | tf_op jit(solution)/shard_map/ppermute | solution.py:676
  6.0 1.7 %collective-permute-start.1 = (bf16[320,1280]{1,0:T(8,128)(2,1)}, bf16[320,1280]{1,0:T(8,128)(2,1)}, u32[]{:S(2)}, u32[]{:S(2)}) collective-permute-start(bf16[320,1280]{1,0:T(8,128)(2,1)} %prepare.1.payload_ref.refs_0_), channel_id=1, source_target_pairs={{4,8},{8,4},{5,9},{9,5},{6,10},{10,6},{7,11},{11,7},{20,24},{24,20... | collective-permute-start | bytes 2457608 | tf_op jit(solution)/shard_map/ppermute | solution.py:676
  7.7 3.6 %gather_blocks.1 = bf16[16,256,256]{2,1,0:T(8,128)(2,1)} custom-call(s32[4]{0:T(128)} %refs_0_.9, s32[4,32]{1,0:T(4,128)} %refs_1_.9, s32[4,32]{1,0:T(4,128)} %refs_2_.9, bf16[32,256,256]{2,1,0:T(8,128)(2,1)} %refs_7_.1, bf16[32,256,256]{2,1,0:T(8,128)(2,1)} %refs_8_.1), custom_call_target="tpu_custom_call" | custom-call | tf_op jit(solution)/shard_map/gather_blocks/pallas_call | solution.py:680
  11.3 5.3 %collective-permute-start.4 = (bf16[16,256,256]{2,1,0:T(8,128)(2,1)}, bf16[16,256,256]{2,1,0:T(8,128)(2,1)}, u32[]{:S(2)}, u32[]{:S(2)}) collective-permute-start(bf16[16,256,256]{2,1,0:T(8,128)(2,1)} %gather_blocks.1), channel_id=1, source_target_pairs={{0,4},{12,8},{1,5},{13,9},{2,6},{14,10},{3,7},{15,11},{16,20},{28,... | collective-permute-start | bytes 6291464 | tf_op jit(solution)/shard_map/ppermute | solution.py:676
  16.5 5.8 %own_part.1 = (f32[256,1280]{1,0:T(8,128)}, f32[8,1280]{1,0:T(8,128)}) custom-call(s32[4]{0:T(128)} %refs_0_.9, s32[4,32]{1,0:T(4,128)} %refs_1_.9, s32[4,32]{1,0:T(4,128)} %refs_2_.9, bf16[320,1280]{1,0:T(8,128)(2,1)} %prepare.1.payload_ref.refs_0_, bf16[160,256]{1,0:T(8,128)(2,1)} %bitcast.7, bf16[160,256]{1,0:T(8,128)(2,1)} %bitcast.9, ...), custom_call_target="tpu_custom_call" | custom-call | flops 5368709120 | bytes 1280 | tf_op jit(solution)/shard_map/own_part/pallas_call | solution.py:577
  22.3 2.6 %collective-permute-done.refs_4_.refs_3_.refs_1_ = bf16[320,1280]{1,0:T(8,128)(2,1)} collective-permute-done((bf16[320,1280]{1,0:T(8,128)(2,1)}, bf16[320,1280]{1,0:T(8,128)(2,1)}, u32[]{:S(2)}, u32[]{:S(2)}) %collective-permute-start) | collective-permute-done | bytes 819232 | tf_op jit(solution)/shard_map/ppermute | solution.py:676
  25.0 0.0 collective-permute-done.1.refs_3_.refs_2_
  25.0 1.3 %collective-permute-start.3 = (bf16[320,1280]{1,0:T(8,128)(2,1)}, bf16[320,1280]{1,0:T(8,128)(2,1)}, u32[]{:S(2)}, u32[]{:S(2)}) collective-permute-start(bf16[320,1280]{1,0:T(8,128)(2,1)} %collective-permute-done.1.refs_3_.refs_2_), channel_id=1, source_target_pairs={{4,0},{8,12},{5,1},{9,13},{6,2},{10,14},{7,3},{11,15},{20,16},{24,... | collective-permute-start | bytes 2457608 | tf_op jit(solution)/shard_map/ppermute | solution.py:676
  26.3 1.6 %collective-permute-start.2 = (bf16[320,1280]{1,0:T(8,128)(2,1)}, bf16[320,1280]{1,0:T(8,128)(2,1)}, u32[]{:S(2)}, u32[]{:S(2)}) collective-permute-start(bf16[320,1280]{1,0:T(8,128)(2,1)} %collective-permute-done.refs_4_.refs_3_.refs_1_), channel_id=1, source_target_pairs={{4,8},{8,4},{5,9},{9,5},{6,10},{10,6},{7,11},{11,7},{20,24},{24,20... | collective-permute-start | bytes 2457608 | tf_op jit(solution)/shard_map/ppermute | solution.py:676
  27.8 10.6 %other_part.5 = bf16[272,1280]{1,0:T(8,128)(2,1)} custom-call(s32[4]{0:T(128)} %refs_0_.9, s32[4,32]{1,0:T(4,128)} %refs_1_.9, s32[4,32]{1,0:T(4,128)} %refs_2_.9, bf16[320,1280]{1,0:T(8,128)(2,1)} %collective-permute-done.1.refs_3_.refs_2_, bf16[320,1280]{1,0:T(8,128)(2,1)} %collective-permute-done.refs_4_.refs_3_.refs_1_, bf16[32,256,256]{2,1,0:T(8,128)(2,1)} %refs_7_.1, ...), custom_call_target="tpu_custom_call" | custom-call | flops 5368709120 | bytes 1280 | tf_op jit(solution)/shard_map/other_part/pallas_call | solution.py:606
  38.4 0.9 other_part.6
  39.3 1.6 %collective-permute-start.5 = (bf16[272,1280]{1,0:T(8,128)(2,1)}, bf16[272,1280]{1,0:T(8,128)(2,1)}, u32[]{:S(2)}, u32[]{:S(2)}) collective-permute-start(bf16[272,1280]{1,0:T(8,128)(2,1)} %other_part.5), channel_id=1, source_target_pairs={{4,8},{8,4},{5,9},{9,5},{6,10},{10,6},{7,11},{11,7},{20,24},{24,20... | collective-permute-start | bytes 2088968 | tf_op jit(solution)/shard_map/ppermute | solution.py:676
  40.9 1.3 %collective-permute-start.7 = (bf16[272,1280]{1,0:T(8,128)(2,1)}, bf16[272,1280]{1,0:T(8,128)(2,1)}, u32[]{:S(2)}, u32[]{:S(2)}) collective-permute-start(bf16[272,1280]{1,0:T(8,128)(2,1)} %other_part.6), channel_id=1, source_target_pairs={{4,0},{8,12},{5,1},{9,13},{6,2},{10,14},{7,3},{11,15},{20,16},{24,... | collective-permute-start | bytes 2088968 | tf_op jit(solution)/shard_map/ppermute | solution.py:676
  42.2 6.1 %collective-permute-done.3.refs_3_.refs_4_ = bf16[320,1280]{1,0:T(8,128)(2,1)} collective-permute-done((bf16[320,1280]{1,0:T(8,128)(2,1)}, bf16[320,1280]{1,0:T(8,128)(2,1)}, u32[]{:S(2)}, u32[]{:S(2)}) %collective-permute-start.3) | collective-permute-done | bytes 819232 | tf_op jit(solution)/shard_map/ppermute | solution.py:676
  48.3 6.2 %other_part.7 = bf16[272,1280]{1,0:T(8,128)(2,1)} custom-call(s32[4]{0:T(128)} %refs_0_.9, s32[4,32]{1,0:T(4,128)} %refs_1_.9, s32[4,32]{1,0:T(4,128)} %refs_2_.9, bf16[320,1280]{1,0:T(8,128)(2,1)} %collective-permute-done.3.refs_3_.refs_4_, bf16[32,256,256]{2,1,0:T(8,128)(2,1)} %refs_7_.1, bf16[32,256,256]{2,1,0:T(8,128)(2,1)} %refs_8_.1), custom_call_target="tpu_custom_call" | custom-call | flops 5368709120 | bytes 1280 | tf_op jit(solution)/shard_map/other_part/pallas_call | solution.py:606
  54.5 6.9 %collective-permute-start.6 = (bf16[272,1280]{1,0:T(8,128)(2,1)}, bf16[272,1280]{1,0:T(8,128)(2,1)}, u32[]{:S(2)}, u32[]{:S(2)}) collective-permute-start(bf16[272,1280]{1,0:T(8,128)(2,1)} %other_part.7), channel_id=1, source_target_pairs={{0,8},{12,4},{1,9},{13,5},{2,10},{14,6},{3,11},{15,7},{16,24},{28,... | collective-permute-start | bytes 2088968 | tf_op jit(solution)/shard_map/ppermute | solution.py:676
  61.5 0.9 other_part.8
  62.4 1.3 %collective-permute-start.10 = (bf16[64,1280]{1,0:T(8,128)(2,1)}, bf16[64,1280]{1,0:T(8,128)(2,1)S(1)}, u32[]{:S(2)}, u32[]{:S(2)}) collective-permute-start(bf16[64,1280]{1,0:T(8,128)(2,1)} %get-tuple-element.50), channel_id=1, source_target_pairs={{4,0},{8,12},{5,1},{9,13},{6,2},{10,14},{7,3},{11,15},{20,16},{24,... | collective-permute-start | bytes 491528 | tf_op jit(solution)/shard_map/ppermute | solution.py:676
  63.7 6.2 %collective-permute-done.4.refs_4_ = bf16[16,256,256]{2,1,0:T(8,128)(2,1)} collective-permute-done((bf16[16,256,256]{2,1,0:T(8,128)(2,1)}, bf16[16,256,256]{2,1,0:T(8,128)(2,1)}, u32[]{:S(2)}, u32[]{:S(2)}) %collective-permute-start.4) | collective-permute-done | bytes 2097184 | tf_op jit(solution)/shard_map/ppermute | solution.py:676
  69.9 5.2 %collective-permute-start.9 = (bf16[272,1280]{1,0:T(8,128)(2,1)}, bf16[272,1280]{1,0:T(8,128)(2,1)}, u32[]{:S(2)}, u32[]{:S(2)}) collective-permute-start(bf16[272,1280]{1,0:T(8,128)(2,1)} %other_part.5), channel_id=1, source_target_pairs={{0,4},{12,8},{1,5},{13,9},{2,6},{14,10},{3,7},{15,11},{16,20},{28,... | collective-permute-start | bytes 2088968 | tf_op jit(solution)/shard_map/ppermute | solution.py:676
  75.1 0.9 other_part.9
  76.1 0.0 collective-permute-done.10.refs_5_
  76.1 0.0 copy-start
  76.1 1.3 %collective-permute-start.8 = (bf16[272,1280]{1,0:T(8,128)(2,1)}, bf16[272,1280]{1,0:T(8,128)(2,1)}, u32[]{:S(2)}, u32[]{:S(2)}) collective-permute-start(bf16[272,1280]{1,0:T(8,128)(2,1)} %other_part.9), channel_id=1, source_target_pairs={{4,12},{8,0},{5,13},{9,1},{6,14},{10,2},{7,15},{11,3},{20,28},{24,... | collective-permute-start | bytes 2088968 | tf_op jit(solution)/shard_map/ppermute | solution.py:676
  77.4 2.6 %push.1 = (bf16[2,160,256]{2,1,0:T(8,128)(2,1)}, bf16[2,160,256]{2,1,0:T(8,128)(2,1)}) custom-call(s32[4]{0:T(128)} %owner_ref.1, bf16[320,1280]{1,0:T(8,128)(2,1)} %prepare.1.payload_ref.refs_0_, bf16[320,1280]{1,0:T(8,128)(2,1)} %collective-permute-done.refs_4_.refs_3_.refs_1_, bf16[320,1280]{1,0:T(8,128)(2,1)} %collective-permute-done.1.refs_3_.refs_2_, ...), custom_call_target="tpu_custom_call" | custom-call | tf_op jit(solution)/shard_map/push/pallas_call | solution.py:732
  80.0 0.0 collective-permute-done.5.refs_0_
  80.1 4.8 %collective-permute-done.6.refs_1_ = bf16[272,1280]{1,0:T(8,128)(2,1)} collective-permute-done((bf16[272,1280]{1,0:T(8,128)(2,1)}, bf16[272,1280]{1,0:T(8,128)(2,1)}, u32[]{:S(2)}, u32[]{:S(2)}) %collective-permute-start.6) | collective-permute-done | bytes 696352 | tf_op jit(solution)/shard_map/ppermute | solution.py:676
  84.9 3.6 %combine.1 = (f32[256,1280]{1,0:T(8,128)}, f32[8,1280]{1,0:T(8,128)}) custom-call(f32[256,1280]{1,0:T(8,128)} %get-tuple-element.45.own_ref, f32[8,1280]{1,0:T(8,128)} %get-tuple-element.46.log_ref, bf16[272,1280]{1,0:T(8,128)(2,1)} %collective-permute-done.5.refs_0_, bf16[272,1280]{1,0:T(8,128)(2,1)} %collective-permute-done.6.refs_1_, ...), custom_call_target="tpu_custom_call" | custom-call | bytes 1280 | tf_op jit(solution)/shard_map/combine/pallas_call | solution.py:636
  88.5 10.2 %collective-permute-done.9.inner_ref = bf16[272,1280]{1,0:T(8,128)(2,1)} collective-permute-done((bf16[272,1280]{1,0:T(8,128)(2,1)}, bf16[272,1280]{1,0:T(8,128)(2,1)}, u32[]{:S(2)}, u32[]{:S(2)}) %collective-permute-start.9) | collective-permute-done | bytes 696352 | tf_op jit(solution)/shard_map/ppermute | solution.py:676
  98.7 2.9 %collective-permute-done.8.outer_ref = bf16[272,1280]{1,0:T(8,128)(2,1)} collective-permute-done((bf16[272,1280]{1,0:T(8,128)(2,1)}, bf16[272,1280]{1,0:T(8,128)(2,1)}, u32[]{:S(2)}, u32[]{:S(2)}) %collective-permute-start.8) | collective-permute-done | bytes 696352 | tf_op jit(solution)/shard_map/ppermute | solution.py:676
  101.5 3.3 %final.1 = bf16[160,2048]{1,0:T(8,128)(2,1)} custom-call(f32[256,1280]{1,0:T(8,128)} %get-tuple-element.47.own_ref, f32[8,1280]{1,0:T(8,128)} %get-tuple-element.48.log_ref, bf16[272,1280]{1,0:T(8,128)(2,1)} %collective-permute-done.8.outer_ref, bf16[272,1280]{1,0:T(8,128)(2,1)} %collective-permute-done.9.inner_ref), custom_call_target="tpu_custom_call" | custom-call | tf_op jit(solution)/shard_map/final/pallas_call | solution.py:648
  (3 shorter events, 0.0 us)
Async XLA Ops:
  3.0 22.0 %collective-permute-start = (bf16[320,1280]{1,0:T(8,128)(2,1)}, bf16[320,1280]{1,0:T(8,128)(2,1)}, u32[]{:S(2)}, u32[]{:S(2)}) collective-permute-start(bf16[320,1280]{1,0:T(8,128)(2,1)} %prepare.1.payload_ref.refs_0_), channel_id=1, source_target_pairs={{0,4},{4,0},{8,12},{12,8},{1,5},{5,1},{9,13},{13,9},{2,6},{6,2},{1... | collective-permute-start | bytes 2457608 | tf_op jit(solution)/shard_map/ppermute | solution.py:676
  6.0 19.0 %collective-permute-start.1 = (bf16[320,1280]{1,0:T(8,128)(2,1)}, bf16[320,1280]{1,0:T(8,128)(2,1)}, u32[]{:S(2)}, u32[]{:S(2)}) collective-permute-start(bf16[320,1280]{1,0:T(8,128)(2,1)} %prepare.1.payload_ref.refs_0_), channel_id=1, source_target_pairs={{4,8},{8,4},{5,9},{9,5},{6,10},{10,6},{7,11},{11,7},{20,24},{24,20... | collective-permute-start | bytes 2457608 | tf_op jit(solution)/shard_map/ppermute | solution.py:676
  11.3 58.7 %collective-permute-start.4 = (bf16[16,256,256]{2,1,0:T(8,128)(2,1)}, bf16[16,256,256]{2,1,0:T(8,128)(2,1)}, u32[]{:S(2)}, u32[]{:S(2)}) collective-permute-start(bf16[16,256,256]{2,1,0:T(8,128)(2,1)} %gather_blocks.1), channel_id=1, source_target_pairs={{0,4},{12,8},{1,5},{13,9},{2,6},{14,10},{3,7},{15,11},{16,20},{28,... | collective-permute-start | bytes 6291464 | tf_op jit(solution)/shard_map/ppermute | solution.py:676
  25.0 23.3 %collective-permute-start.3 = (bf16[320,1280]{1,0:T(8,128)(2,1)}, bf16[320,1280]{1,0:T(8,128)(2,1)}, u32[]{:S(2)}, u32[]{:S(2)}) collective-permute-start(bf16[320,1280]{1,0:T(8,128)(2,1)} %collective-permute-done.1.refs_3_.refs_2_), channel_id=1, source_target_pairs={{4,0},{8,12},{5,1},{9,13},{6,2},{10,14},{7,3},{11,15},{20,16},{24,... | collective-permute-start | bytes 2457608 | tf_op jit(solution)/shard_map/ppermute | solution.py:676
  26.3 35.2 %collective-permute-start.2 = (bf16[320,1280]{1,0:T(8,128)(2,1)}, bf16[320,1280]{1,0:T(8,128)(2,1)}, u32[]{:S(2)}, u32[]{:S(2)}) collective-permute-start(bf16[320,1280]{1,0:T(8,128)(2,1)} %collective-permute-done.refs_4_.refs_3_.refs_1_), channel_id=1, source_target_pairs={{4,8},{8,4},{5,9},{9,5},{6,10},{10,6},{7,11},{11,7},{20,24},{24,20... | collective-permute-start | bytes 2457608 | tf_op jit(solution)/shard_map/ppermute | solution.py:676
  39.3 40.7 %collective-permute-start.5 = (bf16[272,1280]{1,0:T(8,128)(2,1)}, bf16[272,1280]{1,0:T(8,128)(2,1)}, u32[]{:S(2)}, u32[]{:S(2)}) collective-permute-start(bf16[272,1280]{1,0:T(8,128)(2,1)} %other_part.5), channel_id=1, source_target_pairs={{4,8},{8,4},{5,9},{9,5},{6,10},{10,6},{7,11},{11,7},{20,24},{24,20... | collective-permute-start | bytes 2088968 | tf_op jit(solution)/shard_map/ppermute | solution.py:676
  40.9 39.2 %collective-permute-start.7 = (bf16[272,1280]{1,0:T(8,128)(2,1)}, bf16[272,1280]{1,0:T(8,128)(2,1)}, u32[]{:S(2)}, u32[]{:S(2)}) collective-permute-start(bf16[272,1280]{1,0:T(8,128)(2,1)} %other_part.6), channel_id=1, source_target_pairs={{4,0},{8,12},{5,1},{9,13},{6,2},{10,14},{7,3},{11,15},{20,16},{24,... | collective-permute-start | bytes 2088968 | tf_op jit(solution)/shard_map/ppermute | solution.py:676
  54.5 30.4 %collective-permute-start.6 = (bf16[272,1280]{1,0:T(8,128)(2,1)}, bf16[272,1280]{1,0:T(8,128)(2,1)}, u32[]{:S(2)}, u32[]{:S(2)}) collective-permute-start(bf16[272,1280]{1,0:T(8,128)(2,1)} %other_part.7), channel_id=1, source_target_pairs={{0,8},{12,4},{1,9},{13,5},{2,10},{14,6},{3,11},{15,7},{16,24},{28,... | collective-permute-start | bytes 2088968 | tf_op jit(solution)/shard_map/ppermute | solution.py:676
  62.4 13.7 %collective-permute-start.10 = (bf16[64,1280]{1,0:T(8,128)(2,1)}, bf16[64,1280]{1,0:T(8,128)(2,1)S(1)}, u32[]{:S(2)}, u32[]{:S(2)}) collective-permute-start(bf16[64,1280]{1,0:T(8,128)(2,1)} %get-tuple-element.50), channel_id=1, source_target_pairs={{4,0},{8,12},{5,1},{9,13},{6,2},{10,14},{7,3},{11,15},{20,16},{24,... | collective-permute-start | bytes 491528 | tf_op jit(solution)/shard_map/ppermute | solution.py:676
  69.9 28.7 %collective-permute-start.9 = (bf16[272,1280]{1,0:T(8,128)(2,1)}, bf16[272,1280]{1,0:T(8,128)(2,1)}, u32[]{:S(2)}, u32[]{:S(2)}) collective-permute-start(bf16[272,1280]{1,0:T(8,128)(2,1)} %other_part.5), channel_id=1, source_target_pairs={{0,4},{12,8},{1,5},{13,9},{2,6},{14,10},{3,7},{15,11},{16,20},{28,... | collective-permute-start | bytes 2088968 | tf_op jit(solution)/shard_map/ppermute | solution.py:676
  76.1 1.3 %copy-start = (bf16[64,1280]{1,0:T(8,128)(2,1)}, bf16[64,1280]{1,0:T(8,128)(2,1)S(1)}, u32[]{:S(2)}) copy-start(bf16[64,1280]{1,0:T(8,128)(2,1)S(1)} %collective-permute-done.10.refs_5_) | copy-start | bytes 491524
  76.1 25.4 %collective-permute-start.8 = (bf16[272,1280]{1,0:T(8,128)(2,1)}, bf16[272,1280]{1,0:T(8,128)(2,1)}, u32[]{:S(2)}, u32[]{:S(2)}) collective-permute-start(bf16[272,1280]{1,0:T(8,128)(2,1)} %other_part.9), channel_id=1, source_target_pairs={{4,12},{8,0},{5,13},{9,1},{6,14},{10,2},{7,15},{11,3},{20,28},{24,... | collective-permute-start | bytes 2088968 | tf_op jit(solution)/shard_map/ppermute | solution.py:676
